TPU v7x, 32 devices: a whole 2x2x4 slice. The times are simulated.
32 devices in a mesh: section: 2 (over core), seq: 4 (over z), dp: 4 (over y, x).
Axes of the slice: x: 2, y: 2, z: 4, core: 2. Of those that a mesh axis runs over, the one named last changes fastest.
Arguments:
- tracks: bfloat16 [32, 2048, 640], P('dp', 'seq')
- species: int32 [32], P('dp'), may hold values from 0 to 1
- batch_order: int32 [8], replicated, may hold values from 0 to 7, each once
- conv_one: bfloat16 [5, 640, 768], P(None, None, 'dp'), may hold values from -0.109375 to 0.109375
- dilated_kernel: bfloat16 [3, 768, 384], P(None, 'dp'), may hold values from -0.125 to 0.125
- point_wise: bfloat16 [384, 768], P(None, 'dp'), may hold values from -0.3125 to 0.3125
- head_human: bfloat16 [768, 5313], P('dp'), may hold values from -0.21875 to 0.21875
- head_mouse: bfloat16 [768, 1643], P('dp'), may hold values from -0.21875 to 0.21875
- bias_human: float32 [5313], replicated, may hold values from -4 to 4
- bias_mouse: float32 [1643], replicated, may hold values from -4 to 4
- gain_one: float32 [640], replicated, may hold values from 0.1 to 1.9
- shift_one: float32 [640], replicated, may hold values from -3 to 3
- gain_two: float32 [768], replicated, may hold values from 0.1 to 1.9
- shift_two: float32 [768], replicated, may hold values from -3 to 3
- gain_three: float32 [384], replicated, may hold values from 0.1 to 1.9
- shift_three: float32 [384], replicated, may hold values from -3 to 3
- cotangent: bfloat16 [32, 1024, 5313], P('dp', 'seq'), may hold values from -6 to 6
Outputs:
- predicted: bfloat16 [32, 1024, 5313], P('dp', ('seq', 'section'))
- grad_input: bfloat16 [32, 2048, 640], P('dp', ('seq', 'section'))
- grad_conv_one: float32 [5, 640, 768], P(None, None, 'dp')
- grad_conv_two: float32 [3, 768, 384], P(None, 'dp')
- grad_point_wise: float32 [384, 768], P(None, 'dp')
- grad_head_human: float32 [768, 5313], P('dp')
- grad_head_mouse: float32 [768, 1643], P('dp')
- grad_bias_human: float32 [5313], replicated
- grad_bias_mouse: float32 [1643], replicated
- grad_gain_one: float32 [640], replicated
- grad_shift_one: float32 [640], replicated
- grad_gain_two: float32 [768], replicated
- grad_shift_two: float32 [768], replicated
- grad_gain_three: float32 [384], replicated
- grad_shift_three: float32 [384], replicated
Inputs may be any that keep to these rules, and one draw needn't show every extreme that they name: `species`: 0 marks a human window, 1 a mouse window. `batch_order`: each of 0 to 7 exactly once.
All inputs are finite; a program needn't handle non-finite values.
Results may differ from a plain program's by a relative error of at most 0.018.
Values may be sent and summed in bfloat16 or wider, within the bound.
A program may use at most 576 MiB of HBM per device.

v0:
```python
import jax
import jax.numpy as jnp
from jax import lax
from jax.sharding import PartitionSpec as P

BRANCH_DILATION = 11
MB = 4


EPS = 1e-05


def padded_2(block, sides, width):
    for axis, dim in sides:
        count = lax.axis_size(axis)
        forward = [(i, i + 1) for i in range(count - 1)]
        backward = [(target, source) for source, target in forward]
        low = lax.ppermute(
            lax.slice_in_dim(block, block.shape[dim] - width, None, axis=dim), axis, forward
        )
        high = lax.ppermute(lax.slice_in_dim(block, 0, width, axis=dim), axis, backward)
        block = jnp.concatenate([low, block, high], axis=dim)
    return block


def swapped(block, axis, distance):
    count = lax.axis_size(axis)
    route = []
    for low in range(count):
        high = low | 1 << distance
        if high != low and high < count:
            route += [(low, high), (high, low)]
    return lax.ppermute(block, axis, route)


def widen_first(value, reach):
    return padded_2(value, (("seq", 1),), reach)


def second_widening(value, reach):
    return padded_2(value, (("seq", 1),), reach)


def fetch_first(conv_one):
    return lax.all_gather(conv_one, "dp", axis=2, tiled=True)


def fetch_second(dilated_kernel, point_wise, head_human, head_mouse):
    return (
        lax.all_gather(dilated_kernel, "dp", axis=1, tiled=True),
        lax.all_gather(point_wise, "dp", axis=1, tiled=True),
        lax.all_gather(head_human, "dp", axis=0, tiled=True),
        lax.all_gather(head_mouse, "dp", axis=0, tiled=True),
    )


def shard_first(convolution_gradient):
    return lax.psum_scatter(
        convolution_gradient.astype(jnp.bfloat16), "dp", scatter_dimension=2, tiled=True
    ).astype(jnp.float32)


def shard_second(grads):
    return (
        lax.psum_scatter(
            grads[0].astype(jnp.bfloat16), "dp", scatter_dimension=1, tiled=True
        ).astype(jnp.float32),
        lax.psum_scatter(
            grads[1].astype(jnp.bfloat16), "dp", scatter_dimension=1, tiled=True
        ).astype(jnp.float32),
        lax.psum_scatter(
            grads[2].astype(jnp.bfloat16), "dp", scatter_dimension=0, tiled=True
        ).astype(jnp.float32),
        lax.psum_scatter(
            grads[3].astype(jnp.bfloat16), "dp", scatter_dimension=0, tiled=True
        ).astype(jnp.float32),
    )


def absorb_first(total, fresh):
    return total + fresh


def absorb_second(totals, fresh):
    return tuple((a + b for a, b in zip(totals, fresh)))


def batch_stats(value):
    count = value.shape[0] * value.shape[1] * lax.axis_size("seq") * lax.axis_size("dp")
    centre = lax.psum(jnp.sum(value, axis=(0, 1)), ("seq", "dp")) / count
    spread = lax.psum(jnp.sum(jnp.square(value - centre), axis=(0, 1)), ("seq", "dp")) / count
    return (centre, lax.rsqrt(spread + EPS))


def norm_apply(value, gain, shift):
    centre, inv_scale = batch_stats(value)
    normed = (value - centre) * inv_scale
    return (centre, inv_scale, normed, normed * gain + shift)


def norm_back(grad_pre, normed, gain, inv_scale):
    count = grad_pre.shape[0] * grad_pre.shape[1] * lax.axis_size("seq") * lax.axis_size("dp")
    local_shift = jnp.sum(grad_pre, axis=(0, 1))
    local_gain = jnp.sum(grad_pre * normed, axis=(0, 1))
    total_shift, total_gain = lax.psum((local_shift, local_gain), ("seq", "dp"))
    grad_value = gain * inv_scale * (grad_pre - total_shift / count - normed * (total_gain / count))
    return (grad_value, local_gain, local_shift)


def apply_convolution(padded, weight, dilation):
    taps = weight.shape[0]
    length = padded.shape[1] - (taps - 1) * dilation
    total = jnp.einsum(
        "wlc,cd->wld", padded[:, 0:length], weight[0], preferred_element_type=jnp.float32
    )
    for tap_index in range(1, taps):
        start = tap_index * dilation
        total = total + jnp.einsum(
            "wlc,cd->wld",
            padded[:, start : start + length],
            weight[tap_index],
            preferred_element_type=jnp.float32,
        )
    return total


def convolution_weight_gradient(padded, grad, dilation, taps):
    length = grad.shape[1]
    parts = []
    for tap_index in range(taps):
        start = tap_index * dilation
        parts.append(
            jnp.einsum(
                "wlc,wld->cd",
                padded[:, start : start + length],
                grad,
                preferred_element_type=jnp.float32,
            )
        )
    return jnp.stack(parts)


def convolution_input_gradient(grad_padded, weight, dilation):
    taps = weight.shape[0]
    length = grad_padded.shape[1] - (taps - 1) * dilation
    total = jnp.zeros((grad_padded.shape[0], length, weight.shape[1]), jnp.float32)
    for tap_index in range(taps):
        start = (taps - 1 - tap_index) * dilation
        total = total + jnp.einsum(
            "wld,cd->wlc",
            grad_padded[:, start : start + length],
            weight[tap_index],
            preferred_element_type=jnp.float32,
        )
    return total


def head_window(
    summed_row, cot_row, species_id, full_human, full_mouse, bias_human, bias_mouse, sums
):

    def apply_head(weight, bias):
        tracks_here = weight.shape[1]
        pre_act = jnp.dot(summed_row, weight, preferred_element_type=jnp.float32) + bias
        grad_pre = (cot_row[:, :tracks_here].astype(jnp.float32) * jax.nn.sigmoid(pre_act)).astype(
            jnp.bfloat16
        )
        grad_row = jnp.einsum("lt,ct->lc", grad_pre, weight, preferred_element_type=jnp.float32)
        grad_weight = jnp.einsum(
            "lc,lt->ct", summed_row, grad_pre, preferred_element_type=jnp.float32
        )
        return (
            jax.nn.softplus(pre_act),
            grad_row,
            grad_weight,
            jnp.sum(grad_pre.astype(jnp.float32), axis=0),
        )

    def human_case(carried):
        output, grad_row, grad_weight, grad_bias = apply_head(full_human, bias_human)
        return (
            output,
            grad_row,
            (carried[0] + grad_weight, carried[1], carried[2] + grad_bias, carried[3]),
        )

    def mouse_case(carried):
        output, grad_row, grad_weight, grad_bias = apply_head(full_mouse, bias_mouse)
        extra = full_human.shape[1] - full_mouse.shape[1]
        output = jnp.pad(output, ((0, 0), (0, extra)))
        return (
            output,
            grad_row,
            (carried[0], carried[1] + grad_weight, carried[2], carried[3] + grad_bias),
        )

    return lax.cond(species_id == 0, human_case, mouse_case, sums)


def select_role(is_first, first_value, second_value):
    return jax.tree.map(lambda a, b: jnp.where(is_first, a, b), first_value, second_value)


def per_device(
    tracks,
    species,
    batch_order,
    conv_one,
    dilated_kernel,
    point_wise,
    head_human,
    head_mouse,
    bias_human,
    bias_mouse,
    gain_one,
    shift_one,
    gain_two,
    shift_two,
    gain_three,
    shift_three,
    cotangent,
):
    bf16 = jnp.bfloat16
    f32 = jnp.float32
    ndp = lax.axis_size("dp")
    win_dev = tracks.shape[0]
    per_batch = win_dev // MB
    out_len = tracks.shape[1] // 2
    full_one = (conv_one.shape[0], conv_one.shape[1], conv_one.shape[2] * ndp)
    full_two = (dilated_kernel.shape[0], dilated_kernel.shape[1] * ndp, dilated_kernel.shape[2])
    full_point = (point_wise.shape[0], point_wise.shape[1] * ndp)
    full_human = (head_human.shape[0] * ndp, head_human.shape[1])
    full_mouse = (head_mouse.shape[0] * ndp, head_mouse.shape[1])
    channels_two = full_one[2]
    reach_one = conv_one.shape[0] // 2
    second_reach_width = dilated_kernel.shape[0] // 2 * BRANCH_DILATION
    is_first = lax.axis_index("section") == 0
    fetched = fetch_second(dilated_kernel, point_wise, head_human, head_mouse)
    weights = (fetch_first(conv_one), fetched[0], fetched[1], fetched[2], fetched[3])
    big = tuple(
        (jnp.zeros(s, f32) for s in (full_one, full_two, full_point, full_human, full_mouse))
    )
    small = tuple(
        (
            jnp.zeros(p.shape, f32)
            for p in (
                gain_one,
                shift_one,
                gain_two,
                shift_two,
                gain_three,
                shift_three,
                bias_human,
                bias_mouse,
            )
        )
    )
    kept = tuple(
        (
            (jnp.zeros(gain_one.shape, f32), jnp.zeros(gain_one.shape, f32))
            for batch_index in range(MB)
        )
    )
    handed = jnp.zeros((per_batch, out_len, channels_two), bf16)
    state = (
        handed,
        jnp.zeros(tracks.shape, bf16),
        jnp.zeros((win_dev, out_len, head_human.shape[1]), bf16),
        big,
        small,
        kept,
    )
    for tick_index in range(MB + 2):

        def first_step(current, tick_index=tick_index, handed=handed):
            outgoing, grad_input, predicted, big, small, kept = current
            outgoing = jnp.zeros_like(outgoing)
            full_convolution = weights[0]
            if tick_index >= 2:
                batch_index = tick_index - 2
                rows = batch_order[batch_index * per_batch : (batch_index + 1) * per_batch]
                inputs = jnp.take(tracks, rows, axis=0).astype(f32)
                centre, inv_scale = kept[batch_index]
                normed = (inputs - centre) * inv_scale
                activation, gelu_back = jax.vjp(jax.nn.gelu, normed * gain_one + shift_one)
                padded = widen_first(activation.astype(bf16), reach_one)
                convolution_gradient = jnp.repeat(handed * jnp.asarray(0.5, bf16), 2, axis=1)
                fresh = convolution_weight_gradient(
                    padded, convolution_gradient, 1, full_convolution.shape[0]
                )
                grad_act = convolution_input_gradient(
                    widen_first(convolution_gradient, reach_one), full_convolution, 1
                )
                grad_in, local_gain, local_shift = norm_back(
                    gelu_back(grad_act)[0], normed, gain_one, inv_scale
                )
                grad_input = grad_input.at[rows].set(grad_in.astype(bf16))
                big = (absorb_first(big[0], fresh),) + big[1:]
                small = (small[0] + local_gain, small[1] + local_shift) + small[2:]
            if tick_index < MB:
                rows = batch_order[tick_index * per_batch : (tick_index + 1) * per_batch]
                inputs = jnp.take(tracks, rows, axis=0).astype(f32)
                centre, inv_scale, normed, pre_act = norm_apply(inputs, gain_one, shift_one)
                activation = jax.nn.gelu(pre_act).astype(bf16)
                conv_out = apply_convolution(
                    widen_first(activation, reach_one), full_convolution, 1
                )
                outgoing = jnp.mean(
                    conv_out.reshape(per_batch, out_len, 2, channels_two), axis=2
                ).astype(bf16)
                kept = kept[:tick_index] + ((centre, inv_scale),) + kept[tick_index + 1 :]
            return (outgoing, grad_input, predicted, big, small, kept)

        def second_step(current, tick_index=tick_index, handed=handed):
            outgoing, grad_input, predicted, big, small, kept = current
            outgoing = jnp.zeros_like(outgoing)
            if 1 <= tick_index <= MB:
                batch_index = tick_index - 1
                rows = batch_order[batch_index * per_batch : (batch_index + 1) * per_batch]
                kinds = jnp.take(species, rows, axis=0)
                cot_rows = jnp.take(cotangent, rows, axis=0)
                full_convolution, point_full, human_full, mouse_full = (
                    weights[1],
                    weights[2],
                    weights[3],
                    weights[4],
                )
                pooled = handed.astype(f32)
                unused_two, inv_two, normed_two, pre_two = norm_apply(pooled, gain_two, shift_two)
                second_activated, back_two = jax.vjp(jax.nn.gelu, pre_two)
                second_padded_input = second_widening(
                    second_activated.astype(bf16), second_reach_width
                )
                branch_output = apply_convolution(
                    second_padded_input, full_convolution, BRANCH_DILATION
                )
                unused_three, inv_three, normed_three, pre_three = norm_apply(
                    branch_output, gain_three, shift_three
                )
                act_three, back_three = jax.vjp(jax.nn.gelu, pre_three)
                act_three = act_three.astype(bf16)
                lifted = jnp.einsum(
                    "wlc,cd->wld", act_three, point_full, preferred_element_type=f32
                )
                summed = (pooled + lifted).astype(bf16)
                sums = (
                    jnp.zeros(full_human, f32),
                    jnp.zeros(full_mouse, f32),
                    jnp.zeros(bias_human.shape, f32),
                    jnp.zeros(bias_mouse.shape, f32),
                )
                outputs = []
                grad_rows = []
                for window_index in range(per_batch):
                    output, grad_row, sums = head_window(
                        summed[window_index],
                        cot_rows[window_index],
                        kinds[window_index],
                        human_full,
                        mouse_full,
                        bias_human,
                        bias_mouse,
                        sums,
                    )
                    outputs.append(output.astype(bf16))
                    grad_rows.append(grad_row)
                predicted = predicted.at[rows].set(jnp.stack(outputs))
                grad_summed = jnp.stack(grad_rows)
                grad_lift = grad_summed.astype(bf16)
                grad_point = jnp.einsum(
                    "wlc,wld->cd", act_three, grad_lift, preferred_element_type=f32
                )
                grad_act_three = jnp.einsum(
                    "wld,cd->wlc", grad_lift, point_full, preferred_element_type=f32
                )
                branch_output_gradient, gain_sum_three, shift_sum_three = norm_back(
                    back_three(grad_act_three)[0], normed_three, gain_three, inv_three
                )
                branch_output_gradient = branch_output_gradient.astype(bf16)
                convolution_gradient = convolution_weight_gradient(
                    second_padded_input,
                    branch_output_gradient,
                    BRANCH_DILATION,
                    full_convolution.shape[0],
                )
                second_activated_gradient = convolution_input_gradient(
                    second_widening(branch_output_gradient, second_reach_width),
                    full_convolution,
                    BRANCH_DILATION,
                )
                grad_pooled, gain_sum_two, shift_sum_two = norm_back(
                    back_two(second_activated_gradient)[0], normed_two, gain_two, inv_two
                )
                outgoing = (grad_pooled + grad_summed).astype(bf16)
                big = (big[0],) + absorb_second(
                    big[1:], (convolution_gradient, grad_point, sums[0], sums[1])
                )
                small = (
                    small[0],
                    small[1],
                    small[2] + gain_sum_two,
                    small[3] + shift_sum_two,
                    small[4] + gain_sum_three,
                    small[5] + shift_sum_three,
                    small[6] + sums[2],
                    small[7] + sums[3],
                )
            return (outgoing, grad_input, predicted, big, small, kept)

        state = select_role(is_first, first_step(state), second_step(state))
        if tick_index <= MB:
            handed = swapped(state[0], "section", 0)
    outgoing, grad_input, predicted, big, small, kept = state
    first_part = shard_first(big[0])
    second_part = shard_second(big[1:])
    shards = (jnp.where(is_first, first_part, jnp.zeros_like(first_part)),) + tuple(
        (jnp.where(is_first, jnp.zeros_like(part), part) for part in second_part)
    )
    totals = (
        lax.psum(shards[0].astype(jnp.bfloat16), ("section", "seq")).astype(jnp.float32),
        lax.psum(shards[1].astype(jnp.bfloat16), ("section", "seq")).astype(jnp.float32),
        lax.psum(shards[2].astype(jnp.bfloat16), ("section", "seq")).astype(jnp.float32),
        lax.psum(shards[3].astype(jnp.bfloat16), ("section", "seq")).astype(jnp.float32),
        lax.psum(shards[4].astype(jnp.bfloat16), ("section", "seq")).astype(jnp.float32),
    )
    smalls = lax.psum(
        (small[0], small[1], small[2], small[3], small[4], small[5], small[6], small[7]),
        ("section", "seq", "dp"),
    )
    pred_half = predicted.shape[1] // 2
    grad_half = grad_input.shape[1] // 2
    lower_pred, upper_grad = swapped(
        (predicted[:, :pred_half], grad_input[:, grad_half:]), "section", 0
    )
    predicted = jnp.where(is_first, lower_pred, predicted[:, pred_half:])
    grad_input = jnp.where(is_first, grad_input[:, :grad_half], upper_grad)
    return (
        predicted,
        grad_input,
        totals[0],
        totals[1],
        totals[2],
        totals[3],
        totals[4],
        smalls[6],
        smalls[7],
        smalls[0],
        smalls[1],
        smalls[2],
        smalls[3],
        smalls[4],
        smalls[5],
    )


def solution(mesh):
    placed = (
        P("dp", "seq", None),
        P("dp"),
        P(),
        P(None, None, "dp"),
        P(None, "dp", None),
        P(None, "dp"),
        P("dp", None),
        P("dp", None),
        P(),
        P(),
        P(),
        P(),
        P(),
        P(),
        P(),
        P(),
        P("dp", "seq", None),
    )
    return jax.shard_map(
        per_device,
        mesh=mesh,
        in_specs=placed,
        out_specs=(
            P("dp", ("seq", "section"), None),
            P("dp", ("seq", "section"), None),
            P(None, None, "dp"),
            P(None, "dp", None),
            P(None, "dp"),
            P("dp", None),
            P("dp", None),
            P(),
            P(),
            P(),
            P(),
            P(),
            P(),
            P(),
            P(),
        ),
        check_vma=False,
    )
```

profile of v0, /device:TPU:0, one launch (start us, length us, event | category | flops | bytes accessed | tf_op | source)
XLA Modules:
  0.0 2807.1 jit_solution(2300417553326318042)
XLA Ops:
  14.2 44.1 %psum.427 = f32[640]{0:T(1024)S(1)} all-reduce(f32[640]{0:T(1024)S(1)} %convert_reduce_fusion.19), channel_id=1, replica_groups=mesh['section'=2,'seq'=4,'dp'=4] {'seq','dp'}, use_global_device_ids=true, to_apply=%region_1.0 | all-reduce | flops 640 | bytes 5120 | tf_op jit(solution)/shard_map/psum | solution.py:90
  58.9 37.0 %psum.428 = f32[640]{0:T(1024)S(1)} all-reduce(f32[640]{0:T(1024)S(1)} %fusion.66), channel_id=1, replica_groups=mesh['section'=2,'seq'=4,'dp'=4] {'seq','dp'}, use_global_device_ids=true, to_apply=%region_3.0 | all-reduce | flops 640 | bytes 5120 | tf_op jit(solution)/shard_map/psum | solution.py:91
  130.8 14.6 copy.307
  150.4 15.5 copy.308
  275.4 12.4 all_gather.17
  292.4 38.7 %psum.429 = f32[768]{0:T(1024)S(1)} all-reduce(f32[768]{0:T(1024)S(1)} %convert_reduce_fusion.23), channel_id=1, replica_groups=mesh['section'=2,'seq'=4,'dp'=4] {'seq','dp'}, use_global_device_ids=true, to_apply=%region_6.9 | all-reduce | flops 768 | bytes 6144 | tf_op jit(solution)/shard_map/psum | solution.py:90
  331.3 36.6 %psum.430 = f32[768]{0:T(1024)S(1)} all-reduce(f32[768]{0:T(1024)S(1)} %fusion.251), channel_id=1, replica_groups=mesh['section'=2,'seq'=4,'dp'=4] {'seq','dp'}, use_global_device_ids=true, to_apply=%region_8.11 | all-reduce | flops 768 | bytes 6144 | tf_op jit(solution)/shard_map/psum | solution.py:91
  380.3 38.5 %psum.431 = f32[384]{0:T(512)S(1)} all-reduce(f32[384]{0:T(512)S(1)} %get-tuple-element.1078), channel_id=1, replica_groups=mesh['section'=2,'seq'=4,'dp'=4] {'seq','dp'}, use_global_device_ids=true, to_apply=%region_10.13 | all-reduce | flops 384 | bytes 3072 | tf_op jit(solution)/shard_map/psum | solution.py:90
  419.0 37.0 %psum.432 = f32[384]{0:T(512)S(1)} all-reduce(f32[384]{0:T(512)S(1)} %multiply_reduce_fusion.7), channel_id=1, replica_groups=mesh['section'=2,'seq'=4,'dp'=4] {'seq','dp'}, use_global_device_ids=true, to_apply=%region_12.15 | all-reduce | flops 384 | bytes 3072 | tf_op jit(solution)/shard_map/psum | solution.py:91
  459.4 21.5 conditional.8
  481.7 75.2 %conditional.9 = (f32[768,5313]{1,0:T(8,128)}, f32[5313]{0:T(1024)}, f32[1643]{0:T(1024)S(1)}, bf16[1,256,5313]{1,2,0:T(8,128)(2,1)}, f32[1,256,768]{2,1,0:T(8,128)S(1)}, /*index=5*/f32[768,1643]{1,0:T(8,128)}) conditional(s32[]{:T(128)} %bitcast.68, (bf16[256,5313]{1,0:T(8,128)(2,1)S(1)}, bf16[256,768]{1,0:T(8,128)(2,1)}, ...), branch_computations={%region_17.22_spmd, %region_19.24_spmd} | conditional | flops 6293312512 | bytes 148467184 | solution.py:197
  484.7 11.9 convert_reduce_fusion.3
  496.5 17.0 copy.189
  513.5 13.8 bitcast_add_fusion.1
  527.4 16.9 copy.171
  561.7 37.1 %all-reduce.17 = (f32[640]{0:T(1024)S(1)}, f32[384]{0:T(512)S(1)}, f32[384]{0:T(512)S(1)}) all-reduce(f32[640]{0:T(1024)S(1)} %copy-done.209, f32[384]{0:T(512)S(1)} %get-tuple-element.858, f32[384]{0:T(512)S(1)} %get-tuple-element.857), channel_id=1, replica_groups=mesh['section'=2,'seq'=4,'dp'=4] {'seq','dp'}, use_global_device_ids=true, to_apply=%region_23.27 | all-reduce | flops 1408 | bytes 11264 | tf_op jit(solution)/shard_map/psum | solution.py:90
  644.2 73.6 %all-reduce.16 = (f32[640]{0:T(1024)S(1)}, f32[768]{0:T(1024)S(1)}, f32[768]{0:T(1024)S(1)}) all-reduce(f32[640]{0:T(1024)S(1)} %fusion.56, f32[768]{0:T(1024)S(1)} %get-tuple-element.850, f32[768]{0:T(1024)S(1)} %get-tuple-element.849), channel_id=1, replica_groups=mesh['section'=2,'seq'=4,'dp'=4] {'seq','dp'}, use_global_device_ids=true, to_apply=%region_25.29 | all-reduce | flops 2176 | bytes 17408 | tf_op jit(solution)/shard_map/psum | solution.py:91
  767.7 39.6 %psum.439 = f32[768]{0:T(1024)S(1)} all-reduce(f32[768]{0:T(1024)S(1)} %convert_reduce_fusion.22), channel_id=1, replica_groups=mesh['section'=2,'seq'=4,'dp'=4] {'seq','dp'}, use_global_device_ids=true, to_apply=%region_36.40 | all-reduce | flops 768 | bytes 6144 | tf_op jit(solution)/shard_map/psum | solution.py:90
  807.5 36.7 %psum.440 = f32[768]{0:T(1024)S(1)} all-reduce(f32[768]{0:T(1024)S(1)} %fusion.236), channel_id=1, replica_groups=mesh['section'=2,'seq'=4,'dp'=4] {'seq','dp'}, use_global_device_ids=true, to_apply=%region_38.42 | all-reduce | flops 768 | bytes 6144 | tf_op jit(solution)/shard_map/psum | solution.py:91
  856.9 38.5 %psum.441 = f32[384]{0:T(512)S(1)} all-reduce(f32[384]{0:T(512)S(1)} %get-tuple-element.1082), channel_id=1, replica_groups=mesh['section'=2,'seq'=4,'dp'=4] {'seq','dp'}, use_global_device_ids=true, to_apply=%region_40.44 | all-reduce | flops 384 | bytes 3072 | tf_op jit(solution)/shard_map/psum | solution.py:90
  896.7 36.6 %psum.442 = f32[384]{0:T(512)S(1)} all-reduce(f32[384]{0:T(512)S(1)} %multiply_reduce_fusion.5), channel_id=1, replica_groups=mesh['section'=2,'seq'=4,'dp'=4] {'seq','dp'}, use_global_device_ids=true, to_apply=%region_42.46 | all-reduce | flops 384 | bytes 3072 | tf_op jit(solution)/shard_map/psum | solution.py:91
  936.9 52.5 %conditional.10 = (f32[768,5313]{1,0:T(8,128)}, f32[768,1643]{0,1:T(8,128)}, f32[5313]{0:T(1024)}, f32[1643]{0:T(1024)S(1)}, bf16[1,256,5313]{1,2,0:T(8,128)(2,1)}, /*index=5*/f32[1,256,768]{2,1,0:T(8,128)S(1)}) conditional(s32[]{:T(128)} %bitcast.71, (bf16[256,5313]{1,0:T(8,128)(2,1)}, bf16[256,768]{1,0:T(8,128)(2,1)}, ...), branch_computations={%region_43.48_spmd, %region_45.50_spmd} | conditional | flops 6289226752 | bytes 103451160 | solution.py:197
  942.0 11.9 convert_reduce_fusion.5
  963.4 16.9 copy.172
  990.4 76.1 %conditional.11 = (f32[768,5313]{1,0:T(8,128)}, f32[5313]{0:T(1024)}, f32[1643]{0:T(1024)S(1)}, bf16[1,256,5313]{1,2,0:T(8,128)(2,1)}, f32[1,256,768]{2,1,0:T(8,128)S(1)}, /*index=5*/f32[768,1643]{1,0:T(8,128)}) conditional(s32[]{:T(128)} %bitcast.74, (bf16[256,5313]{1,0:T(8,128)(2,1)S(1)}, bf16[256,768]{1,0:T(8,128)(2,1)}, ...), branch_computations={%region_47.52_spmd, %region_49.54_spmd} | conditional | flops 6293312512 | bytes 148212048 | solution.py:197
  993.5 11.3 convert_reduce_fusion.7
  1004.7 17.0 copy.196
  1021.7 13.8 bitcast_add_fusion.3
  1035.6 16.9 copy.173
  1071.4 38.2 %all-reduce.15 = (f32[640]{0:T(1024)}, f32[384]{0:T(512)S(1)}, f32[384]{0:T(512)S(1)}) all-reduce(f32[640]{0:T(1024)S(1)} %copy-done.208, f32[384]{0:T(512)S(1)} %get-tuple-element.856, f32[384]{0:T(512)S(1)} %get-tuple-element.855), channel_id=1, replica_groups=mesh['section'=2,'seq'=4,'dp'=4] {'seq','dp'}, use_global_device_ids=true, to_apply=%region_53.57 | all-reduce | flops 1408 | bytes 11264 | tf_op jit(solution)/shard_map/psum | solution.py:90
  1145.2 17.7 copy.392
  1171.9 73.6 %all-reduce.14 = (f32[640]{0:T(1024)S(1)}, f32[768]{0:T(1024)S(1)}, f32[768]{0:T(1024)S(1)}) all-reduce(f32[640]{0:T(1024)S(1)} %fusion.46, f32[768]{0:T(1024)S(1)} %get-tuple-element.848, f32[768]{0:T(1024)S(1)} %get-tuple-element.847), channel_id=1, replica_groups=mesh['section'=2,'seq'=4,'dp'=4] {'seq','dp'}, use_global_device_ids=true, to_apply=%region_55.59 | all-reduce | flops 2176 | bytes 17408 | tf_op jit(solution)/shard_map/psum | solution.py:91
  1330.5 36.6 %psum.449 = f32[768]{0:T(1024)S(1)} all-reduce(f32[768]{0:T(1024)S(1)} %convert_reduce_fusion.21), channel_id=1, replica_groups=mesh['section'=2,'seq'=4,'dp'=4] {'seq','dp'}, use_global_device_ids=true, to_apply=%region_66.70 | all-reduce | flops 768 | bytes 6144 | tf_op jit(solution)/shard_map/psum | solution.py:90
  1367.4 38.6 %psum.450 = f32[768]{0:T(1024)S(1)} all-reduce(f32[768]{0:T(1024)S(1)} %fusion.221), channel_id=1, replica_groups=mesh['section'=2,'seq'=4,'dp'=4] {'seq','dp'}, use_global_device_ids=true, to_apply=%region_68.72 | all-reduce | flops 768 | bytes 6144 | tf_op jit(solution)/shard_map/psum | solution.py:91
  1417.3 36.7 %psum.451 = f32[384]{0:T(512)S(1)} all-reduce(f32[384]{0:T(512)S(1)} %get-tuple-element.1086), channel_id=1, replica_groups=mesh['section'=2,'seq'=4,'dp'=4] {'seq','dp'}, use_global_device_ids=true, to_apply=%region_70.74 | all-reduce | flops 384 | bytes 3072 | tf_op jit(solution)/shard_map/psum | solution.py:90
  1454.1 38.5 %psum.452 = f32[384]{0:T(512)S(1)} all-reduce(f32[384]{0:T(512)S(1)} %multiply_reduce_fusion.3), channel_id=1, replica_groups=mesh['section'=2,'seq'=4,'dp'=4] {'seq','dp'}, use_global_device_ids=true, to_apply=%region_72.76 | all-reduce | flops 384 | bytes 3072 | tf_op jit(solution)/shard_map/psum | solution.py:91
  1494.5 21.4 conditional.12
  1516.9 27.1 conditional.13
  1547.7 117.8 %all-reduce.13 = (f32[640]{0:T(1024)S(1)}, f32[384]{0:T(512)S(1)}, f32[384]{0:T(512)S(1)}) all-reduce(f32[640]{0:T(1024)S(1)} %copy-done.207, f32[384]{0:T(512)S(1)} %get-tuple-element.854, f32[384]{0:T(512)S(1)} %get-tuple-element.853), channel_id=1, replica_groups=mesh['section'=2,'seq'=4,'dp'=4] {'seq','dp'}, use_global_device_ids=true, to_apply=%region_83.87 | all-reduce | flops 1408 | bytes 11264 | tf_op jit(solution)/shard_map/psum | solution.py:90
  1680.1 71.8 %all-reduce.12 = (f32[640]{0:T(1024)S(1)}, f32[768]{0:T(1024)S(1)}, f32[768]{0:T(1024)S(1)}) all-reduce(f32[640]{0:T(1024)S(1)} %fusion.36, f32[768]{0:T(1024)S(1)} %get-tuple-element.846, f32[768]{0:T(1024)S(1)} %get-tuple-element.845), channel_id=1, replica_groups=mesh['section'=2,'seq'=4,'dp'=4] {'seq','dp'}, use_global_device_ids=true, to_apply=%region_85.89 | all-reduce | flops 2176 | bytes 17408 | tf_op jit(solution)/shard_map/psum | solution.py:91
  1794.9 40.0 %psum.459 = f32[768]{0:T(1024)S(1)} all-reduce(f32[768]{0:T(1024)S(1)} %convert_reduce_fusion.20), channel_id=1, replica_groups=mesh['section'=2,'seq'=4,'dp'=4] {'seq','dp'}, use_global_device_ids=true, to_apply=%region_96.100 | all-reduce | flops 768 | bytes 6144 | tf_op jit(solution)/shard_map/psum | solution.py:90
  1835.2 36.6 %psum.460 = f32[768]{0:T(1024)S(1)} all-reduce(f32[768]{0:T(1024)S(1)} %fusion.206), channel_id=1, replica_groups=mesh['section'=2,'seq'=4,'dp'=4] {'seq','dp'}, use_global_device_ids=true, to_apply=%region_98.102 | all-reduce | flops 768 | bytes 6144 | tf_op jit(solution)/shard_map/psum | solution.py:91
  1884.5 38.6 %psum.461 = f32[384]{0:T(512)S(1)} all-reduce(f32[384]{0:T(512)S(1)} %get-tuple-element.1090), channel_id=1, replica_groups=mesh['section'=2,'seq'=4,'dp'=4] {'seq','dp'}, use_global_device_ids=true, to_apply=%region_100.104 | all-reduce | flops 384 | bytes 3072 | tf_op jit(solution)/shard_map/psum | solution.py:90
  1924.3 36.6 %psum.462 = f32[384]{0:T(512)S(1)} all-reduce(f32[384]{0:T(512)S(1)} %multiply_reduce_fusion.1), channel_id=1, replica_groups=mesh['section'=2,'seq'=4,'dp'=4] {'seq','dp'}, use_global_device_ids=true, to_apply=%region_102.106 | all-reduce | flops 384 | bytes 3072 | tf_op jit(solution)/shard_map/psum | solution.py:91
  1964.5 52.2 %conditional.14 = (f32[768,5313]{1,0:T(8,128)}, f32[768,1643]{0,1:T(8,128)}, f32[5313]{0:T(1024)}, f32[1643]{0:T(1024)S(1)}, bf16[1,256,5313]{1,2,0:T(8,128)(2,1)}, /*index=5*/f32[1,256,768]{2,1,0:T(8,128)S(1)}) conditional(s32[]{:T(128)} %bitcast.83, (bf16[256,5313]{1,0:T(8,128)(2,1)}, bf16[256,768]{1,0:T(8,128)(2,1)}, ...), branch_computations={%region_103.108_spmd, %region_105.110_spmd} | conditional | flops 6289226752 | bytes 103451160 | solution.py:197
  1969.3 11.9 convert_reduce_fusion.13
  1990.6 16.9 copy.176
  2017.7 75.9 %conditional.15 = (f32[768,5313]{1,0:T(8,128)}, f32[5313]{0:T(1024)}, f32[1643]{0:T(1024)S(1)}, bf16[1,256,5313]{1,2,0:T(8,128)(2,1)}, f32[1,256,768]{2,1,0:T(8,128)S(1)}, /*index=5*/f32[768,1643]{1,0:T(8,128)}) conditional(s32[]{:T(128)} %bitcast.86, (bf16[256,5313]{1,0:T(8,128)(2,1)S(1)}, bf16[256,768]{1,0:T(8,128)(2,1)}, ...), branch_computations={%region_107.112_spmd, %region_109.114_spmd} | conditional | flops 6293312512 | bytes 148212048 | solution.py:197
  2020.7 11.2 convert_reduce_fusion.15
  2031.9 17.0 copy.210
  2048.9 13.7 bitcast_add_fusion.7
  2062.7 16.9 copy.177
  2100.3 36.9 %all-reduce.11 = (f32[384]{0:T(512)S(1)}, f32[384]{0:T(512)S(1)}) all-reduce(f32[384]{0:T(512)S(1)} %get-tuple-element.852, f32[384]{0:T(512)S(1)} %get-tuple-element.851), channel_id=1, replica_groups=mesh['section'=2,'seq'=4,'dp'=4] {'seq','dp'}, use_global_device_ids=true, to_apply=%region_130.134 | all-reduce | flops 768 | bytes 6144 | tf_op jit(solution)/shard_map/psum | solution.py:105
  2211.6 42.3 %all-reduce.10 = (f32[768]{0:T(1024)S(1)}, f32[768]{0:T(1024)S(1)}) all-reduce(f32[768]{0:T(1024)S(1)} %get-tuple-element.844, f32[768]{0:T(1024)S(1)} %get-tuple-element.843), channel_id=1, replica_groups=mesh['section'=2,'seq'=4,'dp'=4] {'seq','dp'}, use_global_device_ids=true, to_apply=%region_134.138 | all-reduce | flops 1536 | bytes 12288 | tf_op jit(solution)/shard_map/psum | solution.py:105
  2286.9 13.1 fusion.25
  2316.5 19.8 broadcast_select_fusion.1
  2336.3 17.8 copy.418
  2373.6 19.9 fusion.24
  2409.3 20.0 broadcast_select_fusion
  2433.6 20.9 copy.211
  2490.7 72.3 %all-reduce.9 = (f32[640]{0:T(1024)S(1)}, f32[640]{0:T(1024)S(1)}, f32[640]{0:T(1024)S(1)}, f32[640]{0:T(1024)S(1)}, f32[640]{0:T(1024)S(1)}, /*index=5*/f32[640]{0:T(1024)S(1)}, f32[640]{0:T(1024)S(1)}, f32[640]{0:T(1024)S(1)}) all-reduce(f32[640]{0:T(1024)S(1)} %copy-done.234, ...), channel_id=1, replica_groups=mesh['section'=2,'seq'=4,'dp'=4] {'seq','dp'}, use_global_device_ids=true, to_apply=%region_115.119 | all-reduce | flops 5120 | bytes 40960 | tf_op jit(solution)/shard_map/psum | solution.py:105
  2617.6 38.6 %all-reduce.8 = (f32[5313]{0:T(1024)}, f32[1643]{0:T(1024)}, f32[640]{0:T(1024)}, f32[640]{0:T(1024)}, f32[768]{0:T(1024)}, /*index=5*/f32[768]{0:T(1024)}, f32[384]{0:T(512)}, f32[384]{0:T(512)}) all-reduce(f32[5313]{0:T(1024)S(1)} %add_select_fusion.15, ...), channel_id=1, replica_groups=mesh['section'=2,'seq'=4,'dp'=4] {'section','seq','dp'}, use_global_device_ids=true, to_apply=%region_150.154 | all-reduce | flops 10540 | bytes 84320 | tf_op jit(solution)/shard_map/psum | solution.py:426
  2686.7 20.9 copy.254
  2707.6 82.9 %all-reduce.21.cloned.1.call-done = (bf16[5,640,192]{2,1,0:T(8,128)(2,1)}, bf16[384,192]{1,0:T(8,128)(2,1)}, bf16[3,192,384]{2,1,0:T(8,128)(2,1)}, bf16[192,5313]{1,0:T(8,128)(2,1)}, bf16[192,1643]{1,0:T(8,128)(2,1)}) async-done(((bf16[5,640,192]{2,1,0:T(8,128)(2,1)}, bf16[384,192]{1,0:T(8,128)(2,1)}, bf16[3,192,384]{2,1,0:T(8,128)(2,1)}, bf16[192,5313]{1,0:T(8,128)(2,1)}, bf16[192,1643]{1,0:T(8,128)(2,1)}), ...) | async-done | bytes 4489744 | tf_op jit(solution)/shard_map/psum | solution.py:420
  (1074 shorter events, 983.9 us)
Async XLA Ops:
  7.2 232.5 %all-gather.5.cloned.1.call-start = ((), (), s32[]{:S(2)}) async-start(), calls=%async_computation.5 | async-start | bytes 6144000 | tf_op jit(solution)/shard_map/all_gather | solution.py:45
  7.9 367.3 %all-gather.7.cloned.1.call-start = ((), (), s32[]{:S(2)}) async-start(), calls=%async_computation.6 | async-start | bytes 2211840 | tf_op jit(solution)/shard_map/all_gather | solution.py:50
  8.7 450.6 %all-gather.9.cloned.1.call-start = ((), (), s32[]{:S(2)}) async-start(), calls=%async_computation.7 | async-start | bytes 3194880 | tf_op jit(solution)/shard_map/all_gather | solution.py:53
  9.4 449.9 %all-gather.11.cloned.1.call-start = ((), (), s32[]{:S(2)}) async-start(), calls=%async_computation.8 | async-start | bytes 10321920 | tf_op jit(solution)/shard_map/all_gather | solution.py:52
  10.4 211.8 %copy-start.238 = (s32[2]{0:T(128)}, s32[2]{0:T(128)S(1)}, u32[]{:S(2)}) copy-start(s32[2]{0:T(128)S(1)} %get-tuple-element.1071) | copy-start | bytes 28
  10.4 211.8 %copy-start.236 = (s32[2]{0:T(128)}, s32[2]{0:T(128)S(1)}, u32[]{:S(2)}) copy-start(s32[2]{0:T(128)S(1)} %get-tuple-element.943) | copy-start | bytes 28
  10.4 277.5 %copy-start.198 = (pred[2]{0:T(512)(128)(4,1)}, pred[2]{0:T(512)(128)(4,1)S(1)}, u32[]{:S(2)}) copy-start(pred[2]{0:T(512)(128)(4,1)S(1)} %get-tuple-element.1066) | copy-start | bytes 10
  10.4 279.8 %copy-start.195 = (pred[2]{0:T(512)(128)(4,1)}, pred[2]{0:T(512)(128)(4,1)S(1)}, u32[]{:S(2)}) copy-start(pred[2]{0:T(512)(128)(4,1)S(1)} %get-tuple-element.1070) | copy-start | bytes 10
  10.4 280.8 %copy-start.192 = (pred[2]{0:T(512)(128)(4,1)}, pred[2]{0:T(512)(128)(4,1)S(1)}, u32[]{:S(2)}) copy-start(pred[2]{0:T(512)(128)(4,1)S(1)} %get-tuple-element.942) | copy-start | bytes 10
  100.2 143.7 %collective-permute-start.1 = (bf16[2,2,640]{2,1,0:T(2,128)(2,1)S(1)}, bf16[2,2,640]{2,1,0:T(2,128)(2,1)S(1)}, u32[]{:S(2)}, u32[]{:S(2)}) collective-permute-start(bf16[2,2,640]{2,1,0:T(2,128)(2,1)S(1)} %get-tuple-element.1005), channel_id=1, source_target_pairs={{4,0},{8,4},{12,8},{5,1},{9,5},{13,9},{6,2},{10,6},{14,10},{7,3},{... | collective-permute-start | bytes 15368 | tf_op jit(solution)/shard_map/ppermute | solution.py:21
  101.5 138.2 %collective-permute-start = (bf16[2,2,640]{2,1,0:T(2,128)(2,1)S(1)}, bf16[2,2,640]{2,1,0:T(2,128)(2,1)S(1)}, u32[]{:S(2)}, u32[]{:S(2)}) collective-permute-start(bf16[2,2,640]{2,1,0:T(2,128)(2,1)S(1)} %get-tuple-element.1004), channel_id=1, source_target_pairs={{0,4},{4,8},{8,12},{1,5},{5,9},{9,13},{2,6},{6,10},{10,14},{3,7},{... | collective-permute-start | bytes 15368 | tf_op jit(solution)/shard_map/ppermute | solution.py:18
  106.7 1187.1 %collective-permute-start.39 = (bf16[2,2,640]{2,1,0:T(2,128)(2,1)}, bf16[2,2,640]{2,1,0:T(2,128)(2,1)}, u32[]{:S(2)}, u32[]{:S(2)}) collective-permute-start(bf16[2,2,640]{2,1,0:T(2,128)(2,1)} %get-tuple-element.991), channel_id=1, source_target_pairs={{0,4},{4,8},{8,12},{1,5},{5,9},{9,13},{2,6},{6,10},{10,14},{3,7},{... | collective-permute-start | bytes 15368 | tf_op jit(solution)/shard_map/ppermute | solution.py:18
  109.2 1197.7 %collective-permute-start.40 = (bf16[2,2,640]{2,1,0:T(2,128)(2,1)}, bf16[2,2,640]{2,1,0:T(2,128)(2,1)}, u32[]{:S(2)}, u32[]{:S(2)}) collective-permute-start(bf16[2,2,640]{2,1,0:T(2,128)(2,1)} %get-tuple-element.990), channel_id=1, source_target_pairs={{4,0},{8,4},{12,8},{5,1},{9,5},{13,9},{6,2},{10,6},{14,10},{7,3},{... | collective-permute-start | bytes 15368 | tf_op jit(solution)/shard_map/ppermute | solution.py:21
  110.5 2545.6 %reduce-scatter.18.cloned.1.call-start = ((), (), s32[]{:S(2)}) async-start(), calls=%async_computation.13 | async-start | bytes 737280
  258.3 33.9 %collective-permute-start.2 = (bf16[2,256,768]{2,1,0:T(8,128)(2,1)}, bf16[2,256,768]{2,1,0:T(8,128)(2,1)S(1)}, u32[]{:S(2)}, u32[]{:S(2)}) collective-permute-start(bf16[2,256,768]{2,1,0:T(8,128)(2,1)} %fusion.386), channel_id=1, source_target_pairs={{0,16},{16,0},{1,17},{17,1},{2,18},{18,2},{3,19},{19,3},{4,20},{20... | collective-permute-start | bytes 2359304 | tf_op jit(solution)/shard_map/ppermute | solution.py:33
  369.3 7.5 collective-permute-start.4
  370.6 8.0 collective-permute-start.3
  601.5 38.4 %collective-permute-start.7 = (bf16[2,11,384]{2,1,0:T(8,128)(2,1)}, bf16[2,11,384]{2,1,0:T(8,128)(2,1)S(1)}, u32[]{:S(2)}, u32[]{:S(2)}) collective-permute-start(bf16[2,11,384]{2,1,0:T(8,128)(2,1)} %get-tuple-element.1035), channel_id=1, source_target_pairs={{4,0},{8,4},{12,8},{5,1},{9,5},{13,9},{6,2},{10,6},{14,10},{7,3},{... | collective-permute-start | bytes 50696 | tf_op jit(solution)/shard_map/ppermute | solution.py:21
  602.8 37.7 %collective-permute-start.8 = (bf16[2,11,384]{2,1,0:T(8,128)(2,1)}, bf16[2,11,384]{2,1,0:T(8,128)(2,1)}, u32[]{:S(2)}, u32[]{:S(2)}) collective-permute-start(bf16[2,11,384]{2,1,0:T(8,128)(2,1)} %get-tuple-element.1034), channel_id=1, source_target_pairs={{0,4},{4,8},{8,12},{1,5},{5,9},{9,13},{2,6},{6,10},{10,14},{3,7},{... | collective-permute-start | bytes 50696 | tf_op jit(solution)/shard_map/ppermute | solution.py:18
  722.0 5.3 collective-permute-start.5
  723.3 9.3 collective-permute-start.6
  754.7 12.8 collective-permute-start.9
  761.1 1410.8 %collective-permute-start.41 = (bf16[2,2,640]{2,1,0:T(2,128)(2,1)}, bf16[2,2,640]{2,1,0:T(2,128)(2,1)}, u32[]{:S(2)}, u32[]{:S(2)}) collective-permute-start(bf16[2,2,640]{2,1,0:T(2,128)(2,1)} %get-tuple-element.993), channel_id=1, source_target_pairs={{0,4},{4,8},{8,12},{1,5},{5,9},{9,13},{2,6},{6,10},{10,14},{3,7},{... | collective-permute-start | bytes 15368 | tf_op jit(solution)/shard_map/ppermute | solution.py:18
  766.2 1417.1 %collective-permute-start.42 = (bf16[2,2,640]{2,1,0:T(2,128)(2,1)}, bf16[2,2,640]{2,1,0:T(2,128)(2,1)}, u32[]{:S(2)}, u32[]{:S(2)}) collective-permute-start(bf16[2,2,640]{2,1,0:T(2,128)(2,1)} %get-tuple-element.992), channel_id=1, source_target_pairs={{4,0},{8,4},{12,8},{5,1},{9,5},{13,9},{6,2},{10,6},{14,10},{7,3},{... | collective-permute-start | bytes 15368 | tf_op jit(solution)/shard_map/ppermute | solution.py:21
  846.1 265.5 %copy-start.27 = (bf16[2,256,768]{2,1,0:T(8,128)(2,1)}, bf16[2,256,768]{2,1,0:T(8,128)(2,1)S(1)}, u32[]{:S(2)}) copy-start(bf16[2,256,768]{2,1,0:T(8,128)(2,1)S(1)} %fusion.228) | copy-start | bytes 2359300
  846.1 6.0 collective-permute-start.11
  852.2 3.3 collective-permute-start.10
  1115.1 47.8 %collective-permute-start.14 = (bf16[2,11,384]{2,1,0:T(8,128)(2,1)}, bf16[2,11,384]{2,1,0:T(8,128)(2,1)S(1)}, u32[]{:S(2)}, u32[]{:S(2)}) collective-permute-start(bf16[2,11,384]{2,1,0:T(8,128)(2,1)} %get-tuple-element.1033), channel_id=1, source_target_pairs={{4,0},{8,4},{12,8},{5,1},{9,5},{13,9},{6,2},{10,6},{14,10},{7,3},{... | collective-permute-start | bytes 50696 | tf_op jit(solution)/shard_map/ppermute | solution.py:21
  1162.9 6.0 collective-permute-start.15
  1248.8 4.6 collective-permute-start.12
  1253.4 6.6 collective-permute-start.13
  1260.0 998.8 %collective-permute-start.43 = (bf16[2,2,640]{2,1,0:T(2,128)(2,1)}, bf16[2,2,640]{2,1,0:T(2,128)(2,1)}, u32[]{:S(2)}, u32[]{:S(2)}) collective-permute-start(bf16[2,2,640]{2,1,0:T(2,128)(2,1)} %get-tuple-element.995), channel_id=1, source_target_pairs={{0,4},{4,8},{8,12},{1,5},{5,9},{9,13},{2,6},{6,10},{10,14},{3,7},{... | collective-permute-start | bytes 15368 | tf_op jit(solution)/shard_map/ppermute | solution.py:18
  1293.8 975.2 %collective-permute-start.44 = (bf16[2,2,640]{2,1,0:T(2,128)(2,1)}, bf16[2,2,640]{2,1,0:T(2,128)(2,1)}, u32[]{:S(2)}, u32[]{:S(2)}) collective-permute-start(bf16[2,2,640]{2,1,0:T(2,128)(2,1)} %get-tuple-element.994), channel_id=1, source_target_pairs={{4,0},{8,4},{12,8},{5,1},{9,5},{13,9},{6,2},{10,6},{14,10},{7,3},{... | collective-permute-start | bytes 15368 | tf_op jit(solution)/shard_map/ppermute | solution.py:21
  1306.9 8.0 collective-permute-start.27
  1314.9 8.5 collective-permute-start.28
  1323.4 7.0 collective-permute-start.16
  1407.3 6.0 collective-permute-start.18
  1413.3 3.3 collective-permute-start.17
  1417.3 248.2 %copy-start.37 = (f32[2,256,384]{2,1,0:T(8,128)}, f32[2,256,384]{2,1,0:T(8,128)S(1)}, u32[]{:S(2)}) copy-start(f32[2,256,384]{2,1,0:T(8,128)S(1)} %get-tuple-element.1087) | copy-start | bytes 2359300
  1665.7 5.7 collective-permute-start.21
  1671.4 5.8 collective-permute-start.22
  1756.1 4.0 collective-permute-start.19
  1760.1 6.6 collective-permute-start.20
  1789.7 5.1 collective-permute-start.23
  1873.7 6.0 collective-permute-start.25
  1879.7 3.3 collective-permute-start.24
  2142.1 519.6 %reduce-scatter.10.cloned.1.call-start = ((), (), s32[]{:S(2)}) async-start(), calls=%async_computation.9 | async-start | bytes 2211840 | tf_op jit(solution)/shard_map/reduce_scatter | solution.py:65
  2149.3 514.2 %reduce-scatter.14.cloned.1.call-start = ((), (), s32[]{:S(2)}) async-start(), calls=%async_computation.11 | async-start | bytes 3194880 | tf_op jit(solution)/shard_map/reduce_scatter | solution.py:74
  2165.0 113.6 %collective-permute-start.45 = (bf16[2,2,640]{2,1,0:T(2,128)(2,1)S(1)}, bf16[2,2,640]{2,1,0:T(2,128)(2,1)S(1)}, u32[]{:S(2)}, u32[]{:S(2)}) collective-permute-start(bf16[2,2,640]{2,1,0:T(2,128)(2,1)S(1)} %get-tuple-element.997), channel_id=1, source_target_pairs={{0,4},{4,8},{8,12},{1,5},{5,9},{9,13},{2,6},{6,10},{10,14},{3,7},{... | collective-permute-start | bytes 15368 | tf_op jit(solution)/shard_map/ppermute | solution.py:18
  2171.9 112.4 %collective-permute-start.46 = (bf16[2,2,640]{2,1,0:T(2,128)(2,1)S(1)}, bf16[2,2,640]{2,1,0:T(2,128)(2,1)S(1)}, u32[]{:S(2)}, u32[]{:S(2)}) collective-permute-start(bf16[2,2,640]{2,1,0:T(2,128)(2,1)S(1)} %get-tuple-element.996), channel_id=1, source_target_pairs={{4,0},{8,4},{12,8},{5,1},{9,5},{13,9},{6,2},{10,6},{14,10},{7,3},{... | collective-permute-start | bytes 15368 | tf_op jit(solution)/shard_map/ppermute | solution.py:21
  2189.8 11.9 collective-permute-start.33
  2199.7 465.9 %reduce-scatter.16.cloned.1.call-start = ((), (), s32[]{:S(2)}) async-start(), calls=%async_computation.12 | async-start | bytes 6144000
  2201.7 6.9 collective-permute-start.34
  2257.3 18.2 collective-permute-start.35
  2316.5 357.5 %reduce-scatter.12.cloned.1.call-start = ((), (), s32[]{:S(2)}) async-start(), calls=%async_computation.10 | async-start | bytes 10321920 | tf_op jit(solution)/shard_map/reduce_scatter | solution.py:71
  2354.2 8.9 collective-permute-start.29
  2355.5 7.7 collective-permute-start.30
  2393.5 397.0 %all-reduce.21.cloned.1.call-start = ((), (), s32[]{:S(2)}) async-start(), calls=%async_computation.14 | async-start | bytes 9961472 | tf_op jit(solution)/shard_map/psum | solution.py:420
  2454.5 222.7 %collective-permute-start.26 = (bf16[8,128,5313]{1,0,2:T(8,128)(2,1)}, bf16[8,128,5313]{1,0,2:T(8,128)(2,1)}, u32[]{:S(2)}, u32[]{:S(2)}) collective-permute-start(bf16[8,128,5313]{1,0,2:T(8,128)(2,1)} %copy.211), channel_id=1, source_target_pairs={{0,16},{16,0},{1,17},{17,1},{2,18},{18,2},{3,19},{19,3},{4,20},{20... | collective-permute-start | bytes 32643080 | tf_op jit(solution)/shard_map/ppermute | solution.py:33
  2457.2 7.4 collective-permute-start.31
  2458.5 6.1 collective-permute-start.32
  2473.8 7.7 collective-permute-start.36
  2475.1 6.4 collective-permute-start.37
  2615.5 42.4 %collective-permute-start.38 = (bf16[8,256,640]{2,1,0:T(8,128)(2,1)}, bf16[8,256,640]{2,1,0:T(8,128)(2,1)S(1)}, u32[]{:S(2)}, u32[]{:S(2)}) collective-permute-start(bf16[8,256,640]{2,1,0:T(8,128)(2,1)} %slice.867), channel_id=1, source_target_pairs={{0,16},{16,0},{1,17},{17,1},{2,18},{18,2},{3,19},{19,3},{4,20},{20... | collective-permute-start | bytes 7864328 | tf_op jit(solution)/shard_map/ppermute | solution.py:33
  (276 other events, 6697.4 us)
Sparse Core Ops, SparseCore 0:
  9.9 62.6 all-gather.4
  74.4 32.6 all-gather.6
  108.9 39.0 all-gather.8
  149.8 86.5 all-gather.10
  2142.2 22.8 reduce-scatter.17
  2168.8 33.0 reduce-scatter.9
  2205.3 39.8 reduce-scatter.13
  2316.6 54.6 reduce-scatter.15
  2393.6 82.8 reduce-scatter.11
  2677.3 113.1 all-reduce.20
where the time goes:
time: 2820 us; the launch traced here: 2810 us
  blocking collectives  1300 us (46%)
  local copies, waits for them, and re-layouts  592 us (21%)
  matrix products  414 us (15%)
  other arithmetic  271 us (10%)
  waiting for transfers between devices  104 us (4%)
  starting transfers between devices  102 us (4%)
    psum x12, blocking collectives, batch_stats(): lax.psum(jnp.sum(jnp.square(value - centre), axis=(0, 1)), ('seq', 'dp'))  553 us
    psum x12, blocking collectives, batch_stats(): centre = lax.psum(jnp.sum(value, axis=(0, 1)), ('seq', 'dp')) / count  544 us
    another operation x24, local copies, waits for them, and re-layouts  186 us
    psum x3, blocking collectives, norm_back(): total_shift, total_gain = lax.psum((local_shift, local_gain), ('seq', 'dp'))  152 us
    unnamed x559, local copies, waits for them, and re-layouts  139 us
    psum x1, waiting for transfers between devices, per_device(): lax.psum(shards[0].astype(jnp.bfloat16), ('section', 'seq'))  82.9 us
    select_n x20, other arithmetic, select_role(): jnp.where(is_first, a, b)  81.6 us
    dot_general x32, matrix products, convolution_weight_gradient(): jnp.einsum('wlc,wld->cd', padded[:, start:start + length], grad, preferre...  76.5 us
  transfers between devices with their start and end apart: 57, of which 11 were waited for; matrix products, arithmetic and copies ran while one was open for 44% of the time, Pallas kernels for 0%

commit v1 on v0

v1 whole, which is shorter than its diff:
```python
import functools
import math

import jax
import jax.numpy as jnp
from jax import lax
from jax.experimental import pallas as pl
from jax.experimental.pallas import tpu as pltpu
from jax.sharding import PartitionSpec as P

MESH = pl.DeviceIdType.MESH
DILATION = 11
MB = 4
EPS = 1e-05
EDGE = 16
BLOCK = 1792
LANES = 128
VMEM_LIMIT = 60 * 1024 * 1024
GELU_K = math.sqrt(2.0 / math.pi)
GELU_C = 0.044715
f32 = jnp.float32
bf16 = jnp.bfloat16
VM = pl.BlockSpec(memory_space=pltpu.VMEM)
HBM = pl.BlockSpec(memory_space=pl.ANY)


def params(collective_id=None, limit=VMEM_LIMIT):
    if collective_id is None:
        return pltpu.CompilerParams(vmem_limit_bytes=limit)
    return pltpu.CompilerParams(
        vmem_limit_bytes=limit, collective_id=collective_id, has_side_effects=True
    )


def gelu(u):
    t = jnp.tanh(u * (GELU_K + (GELU_K * GELU_C) * (u * u)))
    h = 0.5 * u
    return h + h * t


def gelu_slope(u):
    uu = u * u
    t = jnp.tanh(u * (GELU_K + (GELU_K * GELU_C) * uu))
    return 0.5 * (1.0 + t) + (0.5 * u) * (1.0 - t * t) * (GELU_K + (3.0 * GELU_K * GELU_C) * uu)


def dot_nn(a, b):
    return jnp.dot(a, b, preferred_element_type=f32)


def dot_nt(a, b):
    return lax.dot_general(a, b, (((1,), (1,)), ((), ())), preferred_element_type=f32)


def dot_tn(a, b):
    return lax.dot_general(a, b, (((0,), (0,)), ((), ())), preferred_element_type=f32)


class Place:
    def __init__(self, shape):
        self.n_sec, self.n_seq, self.n_dp = shape
        self.n_near = self.n_sec * self.n_dp
        self.sec = lax.axis_index("section")
        self.seq = lax.axis_index("seq")
        self.dp = lax.axis_index("dp")
        self.near = self.sec * self.n_dp + self.dp
        n_bins = self.n_seq * self.n_sec
        bins = self.seq * self.n_sec + self.sec
        self.is_first = bins == 0
        self.is_last = bins == n_bins - 1
        low = lax.rem(bins + n_bins - 1, n_bins)
        high = lax.rem(bins + 1, n_bins)
        self.low = self.bin_device(low)
        self.high = self.bin_device(high)
        across = jnp.where(self.sec == 0, low, high)
        self.across = self.bin_device(across)

    def bin_device(self, bins):
        return (lax.rem(bins, self.n_sec), lax.div(bins, self.n_sec), self.dp)

    def near_device(self, rank):
        return (lax.div(rank, self.n_dp), self.seq, lax.rem(rank, self.n_dp))

    def greet(self):
        barrier = pltpu.get_barrier_semaphore()
        for k in range(1, self.n_near):
            rank = lax.rem(self.near + k, self.n_near)
            pl.semaphore_signal(
                barrier, inc=1, device_id=self.near_device(rank), device_id_type=MESH
            )
        for k in range(1, self.n_seq):
            seq = lax.rem(self.seq + k, self.n_seq)
            pl.semaphore_signal(
                barrier, inc=1, device_id=(self.sec, seq, self.dp), device_id_type=MESH
            )
        pl.semaphore_signal(barrier, inc=1, device_id=self.across, device_id_type=MESH)

    def meet(self):
        pl.semaphore_wait(pltpu.get_barrier_semaphore(), self.n_near + self.n_seq - 1)


def halo_copies(place, from_self, arrived, sems):
    up = pltpu.make_async_remote_copy(
        src_ref=from_self[1],
        dst_ref=arrived[0],
        send_sem=sems.at[0],
        recv_sem=sems.at[1],
        device_id=place.high,
        device_id_type=MESH,
    )
    down = pltpu.make_async_remote_copy(
        src_ref=from_self[0],
        dst_ref=arrived[1],
        send_sem=sems.at[2],
        recv_sem=sems.at[3],
        device_id=place.low,
        device_id_type=MESH,
    )
    return up, down


def spread_round(buffer, mine, count, device_of, send, recv):
    copies = []
    for k in range(1, count):
        rank = lax.rem(mine + k, count)
        copy = pltpu.make_async_remote_copy(
            src_ref=buffer.at[mine],
            dst_ref=buffer.at[mine],
            send_sem=send.at[k],
            recv_sem=recv.at[mine],
            device_id=device_of(rank),
            device_id_type=MESH,
        )
        copy.start()
        copies.append((rank, copy))
    for rank, copy in copies:
        pltpu.make_async_remote_copy(
            src_ref=buffer.at[rank],
            dst_ref=buffer.at[rank],
            send_sem=send.at[0],
            recv_sem=recv.at[rank],
            device_id=device_of(rank),
            device_id_type=MESH,
        ).wait_recv()
    for rank, copy in copies:
        copy.wait_send()


def reduce_everywhere(place, value, near_buf, far_buf, sems, combine):
    near_send, near_recv, far_send, far_recv = sems
    near_buf[place.near] = value
    spread_round(
        near_buf, place.near, place.n_near, place.near_device, near_send, near_recv
    )
    far_buf[place.seq] = combine(near_buf, place.n_near, 1)
    spread_round(
        far_buf,
        place.seq,
        place.n_seq,
        lambda seq: (place.sec, seq, place.dp),
        far_send,
        far_recv,
    )
    return combine(far_buf, place.n_seq, place.n_near)


def add_up(buffer, count, weight):
    total = buffer[0]
    for i in range(1, count):
        total = total + buffer[i]
    return total


def merge_stats(rows, buffer, count, weight):
    means = [buffer[i][:MB] for i in range(count)]
    centre = means[0]
    spread = buffer[0][MB:]
    for i in range(1, count):
        centre = centre + means[i]
        spread = spread + buffer[i][MB:]
    centre = centre * (1.0 / count)
    apart = jnp.square(means[0] - centre)
    for i in range(1, count):
        apart = apart + jnp.square(means[i] - centre)
    return jnp.concatenate([centre, spread + apart * float(rows * weight)], axis=0)


def reduce_scratch(shape, rows, columns):
    n_sec, n_seq, n_dp = shape
    near = n_sec * n_dp
    return [
        pltpu.VMEM((near, rows, columns), f32),
        pltpu.VMEM((n_seq, rows, columns), f32),
        pltpu.SemaphoreType.DMA((near,)),
        pltpu.SemaphoreType.DMA((near,)),
        pltpu.SemaphoreType.DMA((n_seq,)),
        pltpu.SemaphoreType.DMA((n_seq,)),
    ]


def local_stats(value):
    count = value.shape[0]
    centre = jnp.sum(value, axis=0, keepdims=True) * (1.0 / count)
    return centre, jnp.sum(jnp.square(value - centre), axis=0, keepdims=True)


def finish_stats(stats, total):
    return jnp.concatenate(
        [stats[:MB], lax.rsqrt(stats[MB:] * (1.0 / total) + EPS)], axis=0
    )


def prepare_kernel(meta, first, second, pairs, low, high, stats, scratch):
    m = pl.program_id(0)
    half = scratch.shape[1]
    start = pl.multiple_of(meta[meta.shape[0] - 1] * half, half)
    values = []
    for i, ref in enumerate((first, second)):
        value = ref[0, pl.ds(start, half), :].astype(f32)
        values.append(value)
        lanes = scratch.shape[0]
        for c in range(lanes):
            scratch[c] = value[:, c * LANES : (c + 1) * LANES]
        both = jnp.concatenate(
            [scratch[c, pl.ds(odd, half // 2, 2), :] for odd in range(2) for c in range(lanes)],
            axis=1,
        )
        pairs[i] = both.astype(bf16)
        low[pl.ds(2 * m + i, 1), :] = both[:1]
        high[pl.ds(2 * m + i, 1), :] = both[half // 2 - 1 :]
    count = 2 * half
    centre = (
        jnp.sum(values[0], axis=0, keepdims=True) + jnp.sum(values[1], axis=0, keepdims=True)
    ) * (1.0 / count)
    spread = jnp.sum(jnp.square(values[0] - centre), axis=0, keepdims=True) + jnp.sum(
        jnp.square(values[1] - centre), axis=0, keepdims=True
    )
    stats[pl.ds(m, 1), :] = centre
    stats[pl.ds(MB + m, 1), :] = spread


def prepare(tracks, meta, half):
    windows, length, channels = tracks.shape
    whole = lambda shape: pl.BlockSpec(shape, lambda m, meta: (0,) * len(shape))
    return pl.pallas_call(
        prepare_kernel,
        grid_spec=pltpu.PrefetchScalarGridSpec(
            num_scalar_prefetch=1,
            grid=(MB,),
            in_specs=[
                pl.BlockSpec((1, length, channels), lambda m, meta: (meta[2 * m], 0, 0)),
                pl.BlockSpec((1, length, channels), lambda m, meta: (meta[2 * m + 1], 0, 0)),
            ],
            out_specs=[
                pl.BlockSpec((2, half // 2, 2 * channels), lambda m, meta: (m, 0, 0)),
                whole((windows, 2 * channels)),
                whole((windows, 2 * channels)),
                whole((2 * MB, channels)),
            ],
            scratch_shapes=[pltpu.VMEM((channels // LANES, half, LANES), f32)],
        ),
        out_shape=[
            jax.ShapeDtypeStruct((windows, half // 2, 2 * channels), bf16),
            jax.ShapeDtypeStruct((windows, 2 * channels), f32),
            jax.ShapeDtypeStruct((windows, 2 * channels), f32),
            jax.ShapeDtypeStruct((2 * MB, channels), f32),
        ],
        compiler_params=params(),
        name="prepare",
    )(meta, tracks, tracks)


def shifted_rows(value, offset, length):
    rows = value.shape[0]
    if offset:
        value = pltpu.roll(value, rows - offset, axis=0)
    return value[:length]


def forward_kernel(
    shape,
    x2,
    edge_low,
    edge_high,
    stats_in,
    gain_one,
    shift_one,
    gain_two,
    shift_two,
    gain_three,
    shift_three,
    w_one,
    w_two,
    w_point,
    u_one,
    u_two,
    pooled,
    pooled_low,
    pooled_high,
    branch,
    branch_low,
    branch_high,
    act_three,
    summed,
    bn_one,
    bn_two,
    bn_three,
    near_one,
    far_one,
    s10,
    s11,
    s12,
    s13,
    near_two,
    far_two,
    s20,
    s21,
    s22,
    s23,
    near_three,
    far_three,
    s30,
    s31,
    s32,
    s33,
    got_low,
    got_high,
    stats_two,
    stats_three,
    halo_sems,
    s_branch_edge_low,
    s_branch_edge_high,
):
    place = Place(shape)
    place.greet()
    windows, length, wide = x2.shape
    channels = wide // 2
    mid = pooled.shape[2]
    small = branch.shape[1]
    parts = shape[0] * shape[1] * shape[2]
    pair = 2 * length
    place.meet()
    up, down = halo_copies(place, (edge_low, edge_high), (got_low, got_high), halo_sems.at[0])
    up.start()
    down.start()
    stats = reduce_everywhere(
        place,
        stats_in[...],
        near_one,
        far_one,
        (s10, s11, s12, s13),
        functools.partial(merge_stats, 4 * length),
    )
    stats = finish_stats(stats, 4 * length * parts)
    bn_one[...] = jnp.concatenate([stats, stats], axis=1)
    up.wait()
    down.wait()

    @pl.loop(0, windows)
    def _(w):
        m = lax.div(w, 2)
        centre = bn_one[pl.ds(m, 1), :]
        scale = bn_one[pl.ds(MB + m, 1), :] * gain_one[...]
        move = shift_one[...]

        def act(value):
            return gelu((value - centre) * scale + move).astype(bf16).astype(f32)

        main = act(x2[w].astype(f32))
        before = jnp.where(place.is_first, 0.0, act(got_low[pl.ds(w, 1), :]))
        after = jnp.where(place.is_last, 0.0, act(got_high[pl.ds(w, 1), :]))
        even, odd = main[:, :channels], main[:, channels:]
        mean = (even + odd) * 0.5
        mean_before = (before[:, :channels] + before[:, channels:]) * 0.5
        mean_after = (after[:, :channels] + after[:, channels:]) * 0.5
        row = lax.broadcasted_iota(jnp.int32, (length, channels), 0)
        top, bottom = row == 0, row == length - 1
        odd_before = jnp.where(top, before[:, channels:], pltpu.roll(odd, 1, axis=0))
        cross = (odd_before + even) * 0.5
        cross_after = (odd[length - 1 :] + after[:, :channels]) * 0.5
        start = pl.multiple_of(w * length, length)
        taps = (
            jnp.where(top, mean_before, pltpu.roll(mean, 1, axis=0)),
            cross,
            mean,
            jnp.where(bottom, cross_after, pltpu.roll(cross, length - 1, axis=0)),
            jnp.where(bottom, mean_after, pltpu.roll(mean, length - 1, axis=0)),
        )
        for t, tap in enumerate(taps):
            u_one[pl.ds(start, length), t * channels : (t + 1) * channels] = tap.astype(bf16)

    @pl.loop(0, MB)
    def _(m):
        start = pl.multiple_of(m * pair, pair)
        value = dot_nt(u_one[pl.ds(start, pair), :], w_one[...]).astype(bf16)
        pooled[pl.ds(2 * m, 2)] = value.reshape(2, length, mid)
        centre, spread = local_stats(value.astype(f32))
        stats_two[pl.ds(m, 1), :] = centre
        stats_two[pl.ds(MB + m, 1), :] = spread

    up, down = halo_copies(
        place,
        (pooled.at[:, pl.ds(0, EDGE), :], pooled.at[:, pl.ds(length - EDGE, EDGE), :]),
        (pooled_low, pooled_high),
        halo_sems.at[1],
    )
    up.start()
    down.start()
    stats = reduce_everywhere(
        place,
        stats_two[...],
        near_two,
        far_two,
        (s20, s21, s22, s23),
        functools.partial(merge_stats, pair),
    )
    bn_two[...] = finish_stats(stats, pair * parts)
    up.wait()
    down.wait()

    @pl.loop(0, windows)
    def _(w):
        m = lax.div(w, 2)
        centre = bn_two[pl.ds(m, 1), :]
        scale = bn_two[pl.ds(MB + m, 1), :] * gain_two[...]
        move = shift_two[...]

        def act(value):
            return gelu((value.astype(f32) - centre) * scale + move)

        ext = jnp.concatenate(
            [
                jnp.where(place.is_first, 0.0, act(pooled_low[w])),
                act(pooled[w]),
                jnp.where(place.is_last, 0.0, act(pooled_high[w])),
            ],
            axis=0,
        )
        start = pl.multiple_of(w * length, length)
        for t in range(3):
            tap = shifted_rows(ext, EDGE + (t - 1) * DILATION, length)
            u_two[pl.ds(start, length), t * mid : (t + 1) * mid] = tap.astype(bf16)

    @pl.loop(0, MB)
    def _(m):
        start = pl.multiple_of(m * pair, pair)
        value = dot_nn(u_two[pl.ds(start, pair), :], w_two[...])
        branch[pl.ds(start, pair), :] = value
        centre, spread = local_stats(value)
        stats_three[pl.ds(m, 1), :] = centre
        stats_three[pl.ds(MB + m, 1), :] = spread
        for i in range(2):
            s_branch_edge_low[2 * m + i] = value[i * length : i * length + EDGE]
            s_branch_edge_high[2 * m + i] = value[(i + 1) * length - EDGE : (i + 1) * length]

    up, down = halo_copies(
        place,
        (s_branch_edge_low, s_branch_edge_high),
        (branch_low, branch_high),
        halo_sems.at[2],
    )
    up.start()
    down.start()
    stats = reduce_everywhere(
        place,
        stats_three[...],
        near_three,
        far_three,
        (s30, s31, s32, s33),
        functools.partial(merge_stats, pair),
    )
    bn_three[...] = finish_stats(stats, pair * parts)

    @pl.loop(0, MB)
    def _(m):
        centre = bn_three[pl.ds(m, 1), :]
        scale = bn_three[pl.ds(MB + m, 1), :] * gain_three[...]
        start = pl.multiple_of(m * pair, pair)
        act = gelu((branch[pl.ds(start, pair), :] - centre) * scale + shift_three[...])
        act = act.astype(bf16)
        act_three[pl.ds(start, pair), :] = act
        lifted = dot_nt(act, w_point[...])
        here = pooled[pl.ds(2 * m, 2)].reshape(pair, mid).astype(f32)
        summed[pl.ds(start, pair), :] = (here + lifted).astype(bf16)

    up.wait()
    down.wait()


def forward(shape, x2, edge_low, edge_high, stats, gains, w_one, w_two, w_point):
    windows, length, wide = x2.shape
    rows = windows * length
    mid, small = w_point.shape
    out = [
        ((rows, w_one.shape[1]), bf16),
        ((rows, w_two.shape[0]), bf16),
        ((windows, length, mid), bf16),
        ((windows, EDGE, mid), bf16),
        ((windows, EDGE, mid), bf16),
        ((rows, small), f32),
        ((windows, EDGE, small), f32),
        ((windows, EDGE, small), f32),
        ((rows, small), bf16),
        ((rows, mid), bf16),
        ((2 * MB, wide), f32),
        ((2 * MB, mid), f32),
        ((2 * MB, small), f32),
    ]
    scratch = (
        reduce_scratch(shape, 2 * MB, wide // 2)
        + reduce_scratch(shape, 2 * MB, mid)
        + reduce_scratch(shape, 2 * MB, small)
    )
    scratch += [
        pltpu.VMEM((windows, wide), f32),
        pltpu.VMEM((windows, wide), f32),
        pltpu.VMEM((2 * MB, mid), f32),
        pltpu.VMEM((2 * MB, small), f32),
        pltpu.SemaphoreType.DMA((3, 4)),
        pltpu.VMEM((windows, EDGE, small), f32),
        pltpu.VMEM((windows, EDGE, small), f32),
    ]
    return pl.pallas_call(
        functools.partial(forward_kernel, shape),
        in_specs=[VM] * 13,
        out_specs=[VM] * len(out),
        out_shape=[jax.ShapeDtypeStruct(*o) for o in out],
        scratch_shapes=scratch,
        compiler_params=params(1),
        name="forward",
    )(x2, edge_low, edge_high, stats, *gains, w_one, w_two, w_point)


def heads_kernel(
    human_tracks,
    mouse_tracks,
    meta,
    summed,
    w_human,
    w_mouse,
    b_human,
    b_mouse,
    cot,
    predicted,
    grad_summed,
    d_human,
    d_mouse,
    db_human,
    db_mouse,
    rows_sorted,
    grad_sorted,
    grad_pre,
):
    j = pl.program_id(0)
    windows, length, block = cot.shape
    pair = 2 * length
    n_pairs = windows // 2
    mid = summed.shape[1]
    n_human = meta[2 * windows]

    @pl.when(j == 0)
    def _():
        grad_sorted[...] = jnp.zeros_like(grad_sorted)

        @pl.loop(0, windows)
        def _(s):
            source = pl.multiple_of(meta[s] * length, length)
            target = pl.multiple_of(s * length, length)
            rows_sorted[pl.ds(target, length), :] = summed[pl.ds(source, length), :]

    column = lax.broadcasted_iota(jnp.int32, (1, block), 1)

    def run(weight, bias, limit, is_mouse, first_pair, last_pair):
        def body(p, carry):
            start = pl.multiple_of(p * pair, pair)
            pre = dot_nn(rows_sorted[pl.ds(start, pair), :], weight[...]) + bias[...]
            decay = jnp.exp(-jnp.abs(pre))
            whole = 1.0 + decay
            inverse = 1.0 / whole
            sigmoid = jnp.where(pre >= 0, inverse, decay * inverse)
            logs = jnp.where(decay < 2.0**-11, decay, jnp.log(whole))
            output = (jnp.maximum(pre, 0.0) + logs).astype(bf16)
            output = jnp.where(column < limit, output, jnp.zeros_like(output))
            for i in range(2):
                s = 2 * p + i
                window = meta[windows + s]
                mine = s >= n_human if is_mouse else s < n_human
                keep = (column < limit) & mine
                part = slice(i * length, (i + 1) * length)
                grad = jnp.where(keep, cot[window].astype(f32) * sigmoid[part], 0.0)
                grad_pre[pl.ds(pl.multiple_of(s * length, length), length), :] = grad.astype(bf16)

                @pl.when(mine)
                def _():
                    predicted[window] = output[part]

            grad_sorted[pl.ds(start, pair), :] += dot_nt(
                grad_pre[pl.ds(start, pair), :], weight[...]
            )
            return carry

        lax.fori_loop(first_pair, last_pair, body, 0)

    def weight_grads(count, n_used, from_end, d_weight, d_bias):
        for n in range(n_pairs + 1):

            @pl.when(n_used == n)
            def _(n=n):
                if n == 0:
                    d_weight[...] = jnp.zeros_like(d_weight)
                    d_bias[...] = jnp.zeros_like(d_bias)
                else:
                    part = slice((n_pairs - n) * pair, None) if from_end else slice(0, n * pair)
                    grad = grad_pre[part, :]
                    d_weight[...] = dot_tn(rows_sorted[part, :], grad).astype(bf16)
                    d_bias[...] = dot_nn(jnp.ones((8, n * pair), bf16), grad)[:1]

    human_pairs = lax.div(n_human + 1, 2)
    run(w_human, b_human, human_tracks - j * block, False, 0, human_pairs)
    weight_grads(n_pairs, human_pairs, False, d_human, db_human)

    @pl.when(j == 0)
    def _():
        mouse_start = lax.div(n_human, 2)
        run(w_mouse, b_mouse, mouse_tracks, True, mouse_start, n_pairs)
        weight_grads(n_pairs, n_pairs - mouse_start, True, d_mouse, db_mouse)

    @pl.when(j > 0)
    def _():
        def body(s, carry):
            predicted[meta[windows + s]] = jnp.zeros((length, block), bf16)
            return carry

        lax.fori_loop(n_human, windows, body, 0)

    @pl.when(j == pl.num_programs(0) - 1)
    def _():
        @pl.loop(0, windows)
        def _(s):
            source = pl.multiple_of(s * length, length)
            target = pl.multiple_of(meta[s] * length, length)
            grad_summed[pl.ds(target, length), :] = grad_sorted[pl.ds(source, length), :]


def heads(meta, summed, w_heads, b_human, b_mouse, cotangent, mouse_tracks, length):
    windows, _, human_tracks = cotangent.shape
    rows, mid = summed.shape
    blocks = w_heads.shape[1] // BLOCK - 1
    sec_at = 2 * windows + 1
    row_block = pl.BlockSpec((1, BLOCK), lambda j, meta: (0, j))
    row_fixed = pl.BlockSpec((1, BLOCK), lambda j, meta: (0, 0))
    fixed = pl.BlockSpec((rows, mid), lambda j, meta: (0, 0))
    return pl.pallas_call(
        functools.partial(heads_kernel, human_tracks, mouse_tracks),
        grid_spec=pltpu.PrefetchScalarGridSpec(
            num_scalar_prefetch=1,
            grid=(blocks,),
            in_specs=[
                fixed,
                pl.BlockSpec((mid, BLOCK), lambda j, meta: (0, j)),
                pl.BlockSpec((mid, BLOCK), lambda j, meta: (0, blocks), pipeline_mode=pl.Buffered(1)),
                row_block,
                row_fixed,
                pl.BlockSpec((windows, length, BLOCK), lambda j, meta: (0, meta[sec_at], j)),
            ],
            out_specs=[
                pl.BlockSpec((windows, length, BLOCK), lambda j, meta: (0, 0, j)),
                fixed,
                pl.BlockSpec((mid, BLOCK), lambda j, meta: (0, j)),
                pl.BlockSpec((mid, BLOCK), lambda j, meta: (0, 0)),
                row_block,
                row_fixed,
            ],
            scratch_shapes=[
                pltpu.VMEM((rows, mid), bf16),
                pltpu.VMEM((rows, mid), f32),
                pltpu.VMEM((rows, BLOCK), bf16),
            ],
        ),
        out_shape=[
            jax.ShapeDtypeStruct((windows, length, human_tracks), bf16),
            jax.ShapeDtypeStruct((rows, mid), f32),
            jax.ShapeDtypeStruct((mid, blocks * BLOCK), bf16),
            jax.ShapeDtypeStruct((mid, BLOCK), bf16),
            jax.ShapeDtypeStruct((1, blocks * BLOCK), f32),
            jax.ShapeDtypeStruct((1, BLOCK), f32),
        ],
        compiler_params=params(),
        name="heads",
    )(meta, summed, w_heads, w_heads, b_human, b_mouse, cotangent)


def back_three_kernel(
    shape,
    grad_summed,
    act_three,
    branch,
    bn_three,
    gain_three,
    shift_three,
    w_point,
    bias_sums,
    d_point,
    du_three,
    du_low,
    du_high,
    gs_low,
    gs_high,
    sums_three,
    bias_out,
    near,
    far,
    s0,
    s1,
    s2,
    s3,
    near_b,
    far_b,
    b0,
    b1,
    b2,
    b3,
    edge_low,
    edge_high,
    row_low,
    row_high,
    sums,
    halo_sems,
):
    place = Place(shape)
    place.greet()
    rows, mid = grad_summed.shape
    pair = rows // MB
    length = pair // 2

    @pl.loop(0, MB)
    def _(m):
        start = pl.multiple_of(m * pair, pair)
        grad = grad_summed[pl.ds(start, pair), :]
        back = dot_nn(grad.astype(bf16), w_point[...])
        centre = bn_three[pl.ds(m, 1), :]
        xhat = (branch[pl.ds(start, pair), :] - centre) * bn_three[pl.ds(MB + m, 1), :]
        du = gelu_slope(xhat * gain_three[...] + shift_three[...]) * back
        du_three[pl.ds(start, pair), :] = du
        sums[pl.ds(m, 1), :] = jnp.sum(du, axis=0, keepdims=True)
        sums[pl.ds(MB + m, 1), :] = jnp.sum(du * xhat, axis=0, keepdims=True)
        for i in range(2):
            edge_low[2 * m + i] = du[i * length : i * length + EDGE]
            edge_high[2 * m + i] = du[(i + 1) * length - EDGE : (i + 1) * length]
            row_low[pl.ds(2 * m + i, 1), :] = grad[i * length : i * length + 1]
            row_high[pl.ds(2 * m + i, 1), :] = grad[(i + 1) * length - 1 : (i + 1) * length]

    place.meet()
    moves = halo_copies(place, (edge_low, edge_high), (du_low, du_high), halo_sems.at[0])
    moves += halo_copies(place, (row_low, row_high), (gs_low, gs_high), halo_sems.at[1])
    for move in moves:
        move.start()
    bias_out[...] = reduce_everywhere(
        place, bias_sums[...], near_b, far_b, (b0, b1, b2, b3), add_up
    )
    sums_three[...] = reduce_everywhere(place, sums[...], near, far, (s0, s1, s2, s3), add_up)
    d_point[...] = dot_tn(grad_summed[...].astype(bf16), act_three[...]).astype(bf16)
    for move in moves:
        move.wait()


def back_three(shape, windows, grad_summed, act_three, branch, bn_three, gain, move, w_point, bias_sums):
    rows, mid = grad_summed.shape
    small = branch.shape[1]
    out = [
        ((mid, small), bf16),
        ((rows, small), f32),
        ((windows, EDGE, small), f32),
        ((windows, EDGE, small), f32),
        ((windows, mid), f32),
        ((windows, mid), f32),
        ((2 * MB, small), f32),
        (bias_sums.shape, f32),
    ]
    scratch = reduce_scratch(shape, 2 * MB, small) + reduce_scratch(shape, *bias_sums.shape)
    scratch += [
        pltpu.VMEM((windows, EDGE, small), f32),
        pltpu.VMEM((windows, EDGE, small), f32),
        pltpu.VMEM((windows, mid), f32),
        pltpu.VMEM((windows, mid), f32),
        pltpu.VMEM((2 * MB, small), f32),
        pltpu.SemaphoreType.DMA((2, 4)),
    ]
    return pl.pallas_call(
        functools.partial(back_three_kernel, shape),
        in_specs=[VM] * 8,
        out_specs=[VM] * len(out),
        out_shape=[jax.ShapeDtypeStruct(*o) for o in out],
        scratch_shapes=scratch,
        compiler_params=params(2),
        name="back_three",
    )(grad_summed, act_three, branch, bn_three, gain, move, w_point, bias_sums)


def back_two_kernel(
    shape,
    du_three,
    du_low,
    du_high,
    sums_three,
    branch,
    branch_low,
    branch_high,
    bn_three,
    gain_three,
    u_two,
    w_two,
    pooled,
    bn_two,
    gain_two,
    shift_two,
    d_two,
    du_two,
    row_low_out,
    row_high_out,
    sums_two,
    near,
    far,
    s0,
    s1,
    s2,
    s3,
    row_low,
    row_high,
    sums,
    grad_branch,
    halo_sems,
):
    place = Place(shape)
    place.greet()
    windows, length, mid = pooled.shape
    parts = shape[0] * shape[1] * shape[2]
    pair = 2 * length
    scale = 1.0 / (pair * parts)
    taps = w_two.shape[0] // mid

    @pl.loop(0, MB)
    def _(m):
        start = pl.multiple_of(m * pair, pair)
        centre = bn_three[pl.ds(m, 1), :]
        inverse = bn_three[pl.ds(MB + m, 1), :]
        factor = gain_three[...] * inverse
        mean_du = sums_three[pl.ds(m, 1), :] * scale
        mean_dx = sums_three[pl.ds(MB + m, 1), :] * scale

        def back(du, value):
            xhat = (value - centre) * inverse
            return factor * (du - mean_du - xhat * mean_dx)

        main = back(du_three[pl.ds(start, pair), :], branch[pl.ds(start, pair), :])
        grad_branch[pl.ds(start, pair), :] = main.astype(bf16)
        pieces = []
        for i in range(2):
            w = 2 * m + i
            low = jnp.where(place.is_first, 0.0, back(du_low[w], branch_low[w]))
            high = jnp.where(place.is_last, 0.0, back(du_high[w], branch_high[w]))
            pieces += [low, main[i * length : (i + 1) * length], high]
        ext = jnp.concatenate(pieces, axis=0).astype(bf16)
        span = length + 2 * EDGE
        through = [dot_nt(ext, w_two[t * mid : (t + 1) * mid, :]) for t in range(taps)]
        centre_two = bn_two[pl.ds(m, 1), :]
        inverse_two = bn_two[pl.ds(MB + m, 1), :]
        total_du = jnp.zeros((1, mid), f32)
        total_dx = jnp.zeros((1, mid), f32)
        for i in range(2):
            w = 2 * m + i
            grad = jnp.zeros((length, mid), f32)
            for t in range(taps):
                whole = through[t][i * span : (i + 1) * span]
                grad = grad + shifted_rows(whole, EDGE - (t - 1) * DILATION, length)
            xhat = (pooled[w].astype(f32) - centre_two) * inverse_two
            du = gelu_slope(xhat * gain_two[...] + shift_two[...]) * grad
            du_two[w] = du
            total_du = total_du + jnp.sum(du, axis=0, keepdims=True)
            total_dx = total_dx + jnp.sum(du * xhat, axis=0, keepdims=True)
            row_low[pl.ds(w, 1), :] = du[:1]
            row_high[pl.ds(w, 1), :] = du[length - 1 :]
        sums[pl.ds(m, 1), :] = total_du
        sums[pl.ds(MB + m, 1), :] = total_dx

    place.meet()
    moves = halo_copies(place, (row_low, row_high), (row_low_out, row_high_out), halo_sems)
    for move in moves:
        move.start()
    sums_two[...] = reduce_everywhere(place, sums[...], near, far, (s0, s1, s2, s3), add_up)
    d_two[...] = dot_tn(u_two[...], grad_branch[...]).astype(bf16)
    for move in moves:
        move.wait()


def back_two(shape, du, sums_three, branch, bn_three, gain_three, u_two, w_two, pooled, bn_two, gain, move):
    windows, length, mid = pooled.shape
    rows, small = branch[0].shape
    out = [
        (w_two.shape, bf16),
        ((windows, length, mid), f32),
        ((windows, mid), f32),
        ((windows, mid), f32),
        ((2 * MB, mid), f32),
    ]
    scratch = reduce_scratch(shape, 2 * MB, mid)
    scratch += [
        pltpu.VMEM((windows, mid), f32),
        pltpu.VMEM((windows, mid), f32),
        pltpu.VMEM((2 * MB, mid), f32),
        pltpu.VMEM((rows, small), bf16),
        pltpu.SemaphoreType.DMA((4,)),
    ]
    return pl.pallas_call(
        functools.partial(back_two_kernel, shape),
        in_specs=[VM] * 15,
        out_specs=[VM] * len(out),
        out_shape=[jax.ShapeDtypeStruct(*o) for o in out],
        scratch_shapes=scratch,
        compiler_params=params(3),
        name="back_two",
    )(*du, sums_three, *branch, bn_three, gain_three, u_two, w_two, pooled, bn_two, gain, move)


def pool_grad_kernel(
    shape,
    du_two,
    du_low,
    du_high,
    sums_two,
    pooled,
    pooled_low,
    pooled_high,
    bn_two,
    gain_two,
    grad_summed,
    gs_low,
    gs_high,
    u_one,
    grad_ext,
    d_one,
    grad_main,
):
    place = Place(shape)
    windows, length, mid = pooled.shape
    parts = shape[0] * shape[1] * shape[2]
    pair = 2 * length
    scale = 1.0 / (pair * parts)

    @pl.loop(0, MB)
    def _(m):
        start = pl.multiple_of(m * pair, pair)
        centre = bn_two[pl.ds(m, 1), :]
        inverse = bn_two[pl.ds(MB + m, 1), :]
        factor = gain_two[...] * inverse
        mean_du = sums_two[pl.ds(m, 1), :] * scale
        mean_dx = sums_two[pl.ds(MB + m, 1), :] * scale

        def back(du, value, extra):
            xhat = (value.astype(f32) - centre) * inverse
            return factor * (du - mean_du - xhat * mean_dx) + extra

        edges = []
        for i in range(2):
            w = 2 * m + i
            at = pl.multiple_of(w * length, length)
            value = back(du_two[w], pooled[w], grad_summed[pl.ds(at, length), :]).astype(bf16)
            grad_ext[m, i * length : (i + 1) * length, :] = value
            grad_main[pl.ds(at, length), :] = value
            low = back(
                du_low[pl.ds(w, 1), :],
                pooled_low[w].astype(f32)[EDGE - 1 :],
                gs_low[pl.ds(w, 1), :],
            )
            high = back(
                du_high[pl.ds(w, 1), :],
                pooled_high[w].astype(f32)[:1],
                gs_high[pl.ds(w, 1), :],
            )
            edges += [jnp.where(place.is_first, 0.0, low), jnp.where(place.is_last, 0.0, high)]
        row = lax.broadcasted_iota(jnp.int32, (EDGE, mid), 0)
        block = jnp.zeros((EDGE, mid), f32)
        for i, edge in enumerate(edges):
            block = jnp.where(row == i, edge, block)
        grad_ext[m, pair : pair + EDGE, :] = block.astype(bf16)

    d_one[...] = dot_tn(grad_main[...], u_one[...]).astype(bf16)


def pool_grad(shape, du, sums_two, pooled, bn_two, gain_two, grad_summed, gs, u_one):
    windows, length, mid = pooled[0].shape
    rows = windows * length
    return pl.pallas_call(
        functools.partial(pool_grad_kernel, shape),
        in_specs=[VM] * 13,
        out_specs=[VM] * 2,
        out_shape=[
            jax.ShapeDtypeStruct((MB, 2 * length + EDGE, mid), bf16),
            jax.ShapeDtypeStruct((mid, u_one.shape[1]), bf16),
        ],
        scratch_shapes=[pltpu.VMEM((rows, mid), bf16)],
        compiler_params=params(),
        name="pool_grad",
    )(*du, sums_two, *pooled, bn_two, gain_two, grad_summed, *gs, u_one)


def back_one_kernel(
    shape,
    grad_ext,
    w_one,
    x2,
    bn_one,
    gain_one,
    shift_one,
    du_one,
    sums_one,
    near,
    far,
    s0,
    s1,
    s2,
    s3,
    sums,
):
    place = Place(shape)
    place.greet()
    windows, length, wide = x2.shape
    channels = wide // 2
    pair = 2 * length

    @pl.loop(0, MB)
    def _(m):
        through = [
            dot_nn(grad_ext[m], w_one[:, t * channels : (t + 1) * channels]) for t in range(5)
        ]
        centre = bn_one[pl.ds(m, 1), :]
        inverse = bn_one[pl.ds(MB + m, 1), :]
        total_du = jnp.zeros((1, wide), f32)
        total_dx = jnp.zeros((1, wide), f32)
        row = lax.broadcasted_iota(jnp.int32, (length, channels), 0)
        top, bottom = row == 0, row == length - 1
        for i in range(2):
            w = 2 * m + i
            main = [t[i * length : (i + 1) * length] for t in through]
            low = [t[pair + 2 * i : pair + 2 * i + 1] for t in through]
            high = [t[pair + 2 * i + 1 : pair + 2 * i + 2] for t in through]
            later = lambda t: jnp.where(bottom, high[t], pltpu.roll(main[t], length - 1, axis=0))
            earlier = lambda t: jnp.where(top, low[t], pltpu.roll(main[t], 1, axis=0))
            mean = later(0) + main[2] + earlier(4)
            cross = main[1] + earlier(3)
            cross_end = high[1] + main[3][length - 1 :]
            cross_later = jnp.where(bottom, cross_end, pltpu.roll(cross, length - 1, axis=0))
            grad = jnp.concatenate([(mean + cross) * 0.5, (mean + cross_later) * 0.5], axis=1)
            xhat = (x2[w].astype(f32) - centre) * inverse
            du = gelu_slope(xhat * gain_one[...] + shift_one[...]) * grad
            du_one[w] = du
            total_du = total_du + jnp.sum(du, axis=0, keepdims=True)
            total_dx = total_dx + jnp.sum(du * xhat, axis=0, keepdims=True)
        sums[pl.ds(m, 1), :] = total_du[:, :channels] + total_du[:, channels:]
        sums[pl.ds(MB + m, 1), :] = total_dx[:, :channels] + total_dx[:, channels:]

    place.meet()
    sums_one[...] = reduce_everywhere(place, sums[...], near, far, (s0, s1, s2, s3), add_up)


def back_one(shape, grad_ext, w_one, x2, bn_one, gain, move):
    windows, length, wide = x2.shape
    out = [((windows, length, wide), f32), ((2 * MB, wide // 2), f32)]
    scratch = reduce_scratch(shape, 2 * MB, wide // 2)
    scratch += [pltpu.VMEM((2 * MB, wide // 2), f32)]
    return pl.pallas_call(
        functools.partial(back_one_kernel, shape),
        in_specs=[VM] * 6,
        out_specs=[VM] * len(out),
        out_shape=[jax.ShapeDtypeStruct(*o) for o in out],
        scratch_shapes=scratch,
        compiler_params=params(4),
        name="back_one",
    )(grad_ext, w_one, x2, bn_one, gain, move)


def input_grad_kernel(total, meta, du, x2, bn_one, sums, gain, out, scratch):
    w = pl.program_id(0)
    m = lax.div(w, 2)
    wide = x2.shape[2]
    channels = wide // 2
    length = x2.shape[1]
    twice = lambda v: jnp.concatenate([v, v], axis=1)
    mean_du = twice(sums[pl.ds(m, 1), :]) * (1.0 / total)
    mean_dx = twice(sums[pl.ds(MB + m, 1), :]) * (1.0 / total)
    centre = bn_one[pl.ds(m, 1), :]
    inverse = bn_one[pl.ds(MB + m, 1), :]
    xhat = (x2[0].astype(f32) - centre) * inverse
    grad = gain[...] * inverse * (du[0] - mean_du - xhat * mean_dx)
    lanes = scratch.shape[0]
    for odd in range(2):
        for c in range(lanes):
            at = odd * channels + c * LANES
            scratch[c, pl.ds(odd, length, 2), :] = grad[:, at : at + LANES]
    for c in range(lanes):
        out[0, :, c * LANES : (c + 1) * LANES] = scratch[c].astype(bf16)


def input_grad(shape, meta, du, x2, bn_one, sums, gain):
    windows, length, wide = x2.shape
    total = 4 * length * shape[0] * shape[1] * shape[2]
    whole = lambda s: pl.BlockSpec(s, lambda w, meta: (0,) * len(s))

    return pl.pallas_call(
        functools.partial(input_grad_kernel, total),
        grid_spec=pltpu.PrefetchScalarGridSpec(
            num_scalar_prefetch=1,
            grid=(windows,),
            in_specs=[
                pl.BlockSpec((1, length, wide), lambda w, meta: (w, 0, 0)),
                pl.BlockSpec((1, length, wide), lambda w, meta: (w, 0, 0)),
                whole(bn_one.shape),
                whole(sums.shape),
                whole(gain.shape),
            ],
            out_specs=pl.BlockSpec(
                (1, 2 * length, wide // 2), lambda w, meta: (meta[w], 0, 0)
            ),
            scratch_shapes=[pltpu.VMEM((wide // 2 // LANES, 2 * length, LANES), f32)],
        ),
        out_shape=jax.ShapeDtypeStruct((windows, 2 * length, wide // 2), bf16),
        compiler_params=params(),
        name="input_grad",
    )(meta, du, x2, bn_one, sums, gain)


def per_device(
    shape,
    tracks,
    species,
    batch_order,
    conv_one,
    dilated_kernel,
    point_wise,
    head_human,
    head_mouse,
    bias_human,
    bias_mouse,
    gain_one,
    shift_one,
    gain_two,
    shift_two,
    gain_three,
    shift_three,
    cotangent,
):
    sec = lax.axis_index("section").astype(jnp.int32)
    windows, seq_bins, channels = tracks.shape
    half = seq_bins // 2
    length = half // 2
    human_tracks, mouse_tracks = head_human.shape[1], head_mouse.shape[1]
    human_wide = -(-human_tracks // BLOCK) * BLOCK
    share = conv_one.shape[2]
    mid = share * shape[2]

    taps_one = conv_one.shape[0]
    shard_one = jnp.transpose(conv_one, (2, 0, 1)).reshape(share, taps_one * channels)
    shard_point = point_wise.T
    shard_heads = jnp.concatenate(
        [
            jnp.pad(head_human, ((0, 0), (0, human_wide - human_tracks))),
            jnp.pad(head_mouse, ((0, 0), (0, BLOCK - mouse_tracks))),
        ],
        axis=1,
    )

    def gathered(shard, axis):
        size = shard.shape[axis] // 2
        part = lax.dynamic_slice_in_dim(shard, sec * size, size, axis)
        return lax.all_gather(part, ("dp", "section"), axis=axis, tiled=True)

    w_one = gathered(shard_one, 0)
    w_two = gathered(dilated_kernel, 1).reshape(-1, dilated_kernel.shape[2])
    w_point = gathered(shard_point, 0)
    w_heads = gathered(shard_heads, 0)

    meta_one = jnp.concatenate([batch_order, sec[None]])
    x2, edge_low, edge_high, stats = prepare(tracks, meta_one, half)
    row = lambda v: v.reshape(1, -1)
    twice = lambda v: jnp.tile(v, 2).reshape(1, -1)
    gains = (
        twice(gain_one),
        twice(shift_one),
        row(gain_two),
        row(shift_two),
        row(gain_three),
        row(shift_three),
    )
    (
        u_one,
        u_two,
        pooled,
        pooled_low,
        pooled_high,
        branch,
        branch_low,
        branch_high,
        act_three,
        summed,
        bn_one,
        bn_two,
        bn_three,
    ) = forward(shape, x2, edge_low, edge_high, stats, gains, w_one, w_two, w_point)

    kinds = species[batch_order]
    is_human = kinds == 0
    n_human = jnp.sum(is_human.astype(jnp.int32))
    place_human = jnp.cumsum(is_human.astype(jnp.int32)) - 1
    place_mouse = n_human + jnp.cumsum(1 - is_human.astype(jnp.int32)) - 1
    target = jnp.where(is_human, place_human, place_mouse)
    positions = jnp.sum(
        jnp.where(target[None, :] == jnp.arange(windows)[:, None], jnp.arange(windows)[None, :], 0),
        axis=1,
    ).astype(jnp.int32)
    meta_two = jnp.concatenate(
        [positions, batch_order[positions], n_human[None], sec[None]]
    ).astype(jnp.int32)
    wide_human = jnp.pad(bias_human, (0, human_wide - human_tracks)).reshape(1, -1)
    wide_mouse = jnp.pad(bias_mouse, (0, BLOCK - mouse_tracks)).reshape(1, -1)
    predicted, grad_summed, d_human, d_mouse, db_human, db_mouse = heads(
        meta_two, summed, w_heads, wide_human, wide_mouse, cotangent, mouse_tracks, length
    )

    bias_sums = jnp.concatenate([db_human, db_mouse], axis=1).reshape(8, -1)
    d_point, du_three, du_low, du_high, gs_low, gs_high, sums_three, bias_out = back_three(
        shape, windows, grad_summed, act_three, branch, bn_three, gains[4], gains[5], w_point, bias_sums
    )
    d_two, du_two, dlow_two, dhigh_two, sums_two = back_two(
        shape,
        (du_three, du_low, du_high),
        sums_three,
        (branch, branch_low, branch_high),
        bn_three,
        gains[4],
        u_two,
        w_two,
        pooled,
        bn_two,
        gains[2],
        gains[3],
    )
    grad_ext, d_one = pool_grad(
        shape,
        (du_two, dlow_two, dhigh_two),
        sums_two,
        (pooled, pooled_low, pooled_high),
        bn_two,
        gains[2],
        grad_summed,
        (gs_low, gs_high),
        u_one,
    )
    du_one, sums_one = back_one(shape, grad_ext, w_one, x2, bn_one, gains[0], gains[1])
    grad_input = input_grad(shape, meta_one, du_one, x2, bn_one, sums_one, gains[0])

    def reduced(grad, axis):
        part = lax.psum_scatter(grad, "dp", scatter_dimension=axis, tiled=True)
        return lax.psum(part, ("section", "seq")).astype(f32)

    r_human = reduced(d_human, 0)[:, :human_tracks]
    r_mouse = reduced(d_mouse, 0)[:, :mouse_tracks]
    r_two = reduced(d_two.reshape((dilated_kernel.shape[0], mid, -1)), 1)
    r_point = reduced(d_point, 0).T
    r_one = jnp.transpose(reduced(d_one, 0).reshape(share, taps_one, channels), (1, 2, 0))
    bias = bias_out.reshape(-1)
    return (
        predicted,
        grad_input,
        r_one,
        r_two,
        r_point,
        r_human,
        r_mouse,
        bias[:human_tracks],
        bias[human_wide : human_wide + mouse_tracks],
        jnp.sum(sums_one[MB:], axis=0),
        jnp.sum(sums_one[:MB], axis=0),
        jnp.sum(sums_two[MB:], axis=0),
        jnp.sum(sums_two[:MB], axis=0),
        jnp.sum(sums_three[MB:], axis=0),
        jnp.sum(sums_three[:MB], axis=0),
    )


def solution(mesh):
    shape = (mesh.shape["section"], mesh.shape["seq"], mesh.shape["dp"])
    placed = (
        P("dp", "seq", None),
        P("dp"),
        P(),
        P(None, None, "dp"),
        P(None, "dp", None),
        P(None, "dp"),
        P("dp", None),
        P("dp", None),
    ) + (P(),) * 8 + (P("dp", "seq", None),)
    return jax.shard_map(
        functools.partial(per_device, shape),
        mesh=mesh,
        in_specs=placed,
        out_specs=(
            P("dp", ("seq", "section"), None),
            P("dp", ("seq", "section"), None),
            P(None, None, "dp"),
            P(None, "dp", None),
            P(None, "dp"),
            P("dp", None),
            P("dp", None),
        )
        + (P(),) * 8,
        check_vma=False,
    )
```

time: 2820 us -> 679 us (0.24)
  blocking collectives: 1300 us -> 14.6 us
  local copies, waits for them, and re-layouts: 592 us -> 64 us
  matrix products: 414 us -> 0 us
  other arithmetic: 271 us -> 14.8 us
  waiting for transfers between devices: 104 us -> 337 us
  Pallas kernels: 0 us -> 223 us
  starting transfers between devices: 102 us -> 0.36 us
    psum x28 -> x0, blocking collectives: 1290 us -> none  [the longest x12 553 us: batch_stats(): lax.psum(jnp.sum(jnp.square(value - centre), axis=(0, 1)), ('seq', 'dp'))]
    dot_general x132 -> x0, matrix products: 414 us -> none  [the longest x32 76.5 us: convolution_weight_gradient(): jnp.einsum('wlc,wld->cd', padded[:, start:start + length], grad, preferre...]
    reduce_scatter x3 -> x5, waiting for transfers between devices: 0.01 us -> 249 us  [reduced(): part = lax.psum_scatter(grad, 'dp', scatter_dimension=axis, tiled=True)]
    pallas_call x0 -> x8, Pallas kernels: none -> 223 us  [the longest x1 59.4 us: heads(): pl.pallas_call(functools.partial(heads_kernel, human_tracks, mouse_tracks...]
    another operation x31 -> x0, local copies, waits for them, and re-layouts: 195 us -> none
    select_n x30 -> x3, other arithmetic: 106 us -> 0.66 us  [the longest x1 0.65 us: per_device(): target = jnp.where(is_human, place_human, place_mouse)]
    ppermute x47 -> x0, starting transfers between devices: 101 us -> none  [the longest x20 71.3 us: padded_2(): lax.ppermute(lax.slice_in_dim(block, block.shape[dim] - width, None, axis...]
    unnamed x559 -> x50, local copies, waits for them, and re-layouts: 139 us -> 50.7 us
  transfers between devices with their start and end apart: 57 -> 9, of which waited for: 11 -> 8; matrix products, arithmetic and copies ran while one was open for 44% -> 10% of each run, Pallas kernels for 0% -> 15%
where the time goes in v1:
time: 679 us; the launch traced here: 668 us
  waiting for transfers between devices  337 us (50%)
  Pallas kernels  223 us (33%)
  local copies, waits for them, and re-layouts  64 us (9%)
  other arithmetic  14.8 us (2%)
  blocking collectives  14.6 us (2%)
  between operations  14.4 us (2%)
    reduce_scatter x5, waiting for transfers between devices, reduced(): part = lax.psum_scatter(grad, 'dp', scatter_dimension=axis, tiled=True)  249 us
    psum x1, waiting for transfers between devices, reduced(): return lax.psum(part, ('section', 'seq')).astype(f32)  62.4 us
    pallas_call x1, Pallas kernels, heads(): pl.pallas_call(functools.partial(heads_kernel, human_tracks, mouse_tracks...  59.4 us
    pallas_call x1, Pallas kernels, forward(): pl.pallas_call(functools.partial(forward_kernel, shape), in_specs=[VM] *...  57.7 us
    unnamed x50, local copies, waits for them, and re-layouts  50.7 us
    pallas_call x1, Pallas kernels, back_one(): pl.pallas_call(functools.partial(back_one_kernel, shape), in_specs=[VM] *...  27.6 us
    pallas_call x1, Pallas kernels, back_three(): pl.pallas_call(functools.partial(back_three_kernel, shape), in_specs=[VM]...  25.5 us
    pallas_call x1, Pallas kernels, back_two(): pl.pallas_call(functools.partial(back_two_kernel, shape), in_specs=[VM] *...  23.3 us
  transfers between devices with their start and end apart: 9, of which 8 were waited for; matrix products, arithmetic and copies ran while one was open for 10% of the time, Pallas kernels for 15%

profile of v1, /device:TPU:0, one launch (start us, length us, event | category | flops | bytes accessed | tf_op | source)
XLA Modules:
  0.0 668.0 jit_solution(3837999244271712801)
XLA Ops:
  7.2 1.0 copy-done
  8.2 0.7 constant_dynamic-slice_fusion
  8.9 0.0 all-gather.4.cloned.1.call-start
  9.0 2.8 copy.42
  11.8 0.3 constant_dynamic-slice_fusion.1
  12.1 1.1 copy.48
  13.4 0.0 all-gather.8.cloned.1.call-start
  13.5 2.4 fusion.2
  15.9 0.0 reduce-scatter.6.cloned.1.call-start
  16.0 0.6 reshape.158.gain_three
  16.5 0.6 reshape.159.shift_three
  17.1 0.6 reshape.156.gain_two
  17.7 0.6 reshape.157.shift_two
  18.3 0.6 gather_fusion
  19.0 0.2 reduce-window.17
  19.1 0.2 reduce-window.16
  19.3 0.6 fusion.4
  20.0 0.7 compare_select_fusion.2
  20.6 0.1 select_reduce_fusion
  20.8 0.6 gather_fusion.1
  21.4 0.6 copy.49
  22.0 0.6 copy.50
  22.6 0.6 reshape.163.b_mouse
  23.2 0.6 reshape.162.b_human
  23.8 28.0 %copy.44.cot = bf16[8,256,5313]{2,1,0:T(8,128)(2,1)} copy(bf16[8,256,5313]{1,0,2:T(8,128)(2,1)} %param.33) | data formatting | bytes 43524096 | tf_op args[16]
  51.9 0.6 pad_add_fusion.1.meta
  52.5 5.8 prepare.1
  58.3 1.2 pad_add_fusion.meta
  59.5 14.6 %all_gather.14.w_point = bf16[768,384]{1,0:T(8,128)(2,1)} all-gather(bf16[96,384]{1,0:T(8,128)(2,1)S(1)} %dynamic-slice_bitcast_fusion), channel_id=1, replica_groups=mesh['section'=2,'seq'=4,'dp'=4] {'dp','section'}, dimensions={0}, use_global_device_ids=true | all-gather | bytes 663552 | tf_op jit(solution)/shard_map/all_gather | solution.py:1175
  74.2 9.8 %all-gather.4.cloned.1.call-done.w_one = bf16[768,3200]{1,0:T(8,128)(2,1)} async-done(((bf16[96,3200]{1,0:T(8,128)(2,1)}), bf16[768,3200]{1,0:T(8,128)(2,1)}) %all-gather.4.cloned.1.call-update) | async-done | bytes 4915216 | tf_op jit(solution)/shard_map/all_gather | solution.py:1175
  84.0 57.7 %forward.1 = (bf16[1024,3200]{1,0:T(8,128)(2,1)}, bf16[1024,2304]{1,0:T(8,128)(2,1)}, bf16[8,128,768]{2,1,0:T(8,128)(2,1)}, bf16[8,16,768]{2,1,0:T(8,128)(2,1)},...) custom-call(bf16[8,128,1280]{2,1,0:T(8,128)(2,1)} %get-tuple-element, ...), custom_call_target="tpu_custom_call" | custom-call | tf_op jit(solution)/shard_map/forward/pallas_call | solution.py:523
  141.7 13.4 %all-gather.8.cloned.1.call-done.w_human.w_mouse = bf16[768,7168]{1,0:T(8,128)(2,1)} async-done(((bf16[96,7168]{1,0:T(8,128)(2,1)}), bf16[768,7168]{1,0:T(8,128)(2,1)}) %all-gather.8.cloned.1.call-update) | async-done | bytes 11010064 | tf_op jit(solution)/shard_map/all_gather | solution.py:1175
  155.1 59.4 %heads.1 = (bf16[8,128,5313]{2,1,0:T(8,128)(2,1)}, f32[1024,768]{1,0:T(8,128)}, bf16[768,5376]{1,0:T(8,128)(2,1)}, bf16[768,1792]{1,0:T(8,128)(2,1)}, f32[1,5376]{1,0:T(1,128)}, /*index=5*/f32[1,1792]{1,0:T(1,128)}) custom-call(s32[18]{0:T(128)} %pad_add_fusion.meta, bf16[1024,768]{1,0:T(8,128)(2,1)} %get-tuple-element.59.summed, ...), custom_call_target="tpu_custom_call" | custom-call | tf_op jit(solution)/shard_map/heads/pallas_call | solution.py:653
  214.5 0.8 maximum_reduce_fusion
  215.3 0.6 reshape.164.bias_sums
  215.9 25.5 %back_three.1 = (bf16[768,384]{1,0:T(8,128)(2,1)}, f32[1024,384]{1,0:T(8,128)}, f32[8,16,384]{2,1,0:T(8,128)}, f32[8,16,384]{2,1,0:T(8,128)}, f32[8,768]{1,0:T(8...) custom-call(f32[1024,768]{1,0:T(8,128)} %get-tuple-element.61.grad_summed, ...), custom_call_target="tpu_custom_call" | custom-call | tf_op jit(solution)/shard_map/back_three/pallas_call | solution.py:789
  241.5 23.3 %back_two.1 = (bf16[2304,384]{1,0:T(8,128)(2,1)}, f32[8,128,768]{2,1,0:T(8,128)}, f32[8,768]{1,0:T(8,128)}, f32[8,768]{1,0:T(8,128)}, f32[8,768]{1,0:T(8,128)}) custom-call(f32[1024,384]{1,0:T(8,128)} %get-tuple-element.67.du_three, f32[8,16,384]{2,1,0:T(8,128)} %get-tuple-element.68.du_low, f32[8,16,384]{2,1,0:T(8,128)} %get-tuple-element.69.du_high, ...), custom_call_target="tpu_custom_call" | custom-call | tf_op jit(solution)/shard_map/back_two/pallas_call | solution.py:914
  264.8 14.4 %pool_grad.1 = (bf16[4,272,768]{2,1,0:T(8,128)(2,1)}, bf16[768,3200]{1,0:T(8,128)(2,1)}) custom-call(f32[8,128,768]{2,1,0:T(8,128)} %get-tuple-element.76.du_two, f32[8,768]{1,0:T(8,128)} %get-tuple-element.77.du_low, f32[8,768]{1,0:T(8,128)} %get-tuple-element.78.du_high, f32[8,768]{1,0:T(8,128)} %get-tuple-element.79.sums_two, ...), custom_call_target="tpu_custom_call" | custom-call | tf_op jit(solution)/shard_map/pool_grad/pallas_call | solution.py:993
  279.2 0.0 reduce-scatter.10.cloned.1.call-start
  279.2 0.5 reduce-scatter.10.cloned.1.call-update
  279.8 0.5 reduce-scatter.8.cloned.1.call-update
  280.4 0.7 reduce-scatter.14.cloned.1.call-update
  281.1 0.7 reduce-scatter.12.cloned.1.call-update
  281.9 55.0 %reduce-scatter.6.cloned.1.call-done = bf16[192,3200]{1,0:T(8,128)(2,1)} async-done(((bf16[768,3200]{1,0:T(8,128)(2,1)}), bf16[192,3200]{1,0:T(8,128)(2,1)}) %reduce-scatter.6.cloned.1.call-update) | async-done | bytes 1228816 | tf_op jit(solution)/shard_map/reduce_scatter | solution.py:1262
  336.9 2.8 copy.45
  339.7 25.0 %reduce-scatter.10.cloned.1.call-done = bf16[192,384]{1,0:T(8,128)(2,1)} async-done(((bf16[768,384]{1,0:T(8,128)(2,1)}), bf16[192,384]{1,0:T(8,128)(2,1)}) %reduce-scatter.10.cloned.1.call-update) | async-done | bytes 147472 | tf_op jit(solution)/shard_map/reduce_scatter | solution.py:1262
  364.7 35.7 %reduce-scatter.8.cloned.1.call-done = bf16[3,192,384]{2,1,0:T(8,128)(2,1)} async-done(((bf16[3,768,384]{2,1,0:T(8,128)(2,1)}), bf16[3,192,384]{2,1,0:T(8,128)(2,1)}) %reduce-scatter.8.cloned.1.call-update) | async-done | bytes 442384 | tf_op jit(solution)/shard_map/reduce_scatter | solution.py:1262
  400.4 44.0 %reduce-scatter.14.cloned.1.call-done = bf16[192,1792]{1,0:T(8,128)(2,1)} async-done(((bf16[768,1792]{1,0:T(8,128)(2,1)}), bf16[192,1792]{1,0:T(8,128)(2,1)}) %reduce-scatter.14.cloned.1.call-update) | async-done | bytes 688144 | tf_op jit(solution)/shard_map/reduce_scatter | solution.py:1262
  444.4 89.4 %reduce-scatter.12.cloned.1.call-done = bf16[192,5376]{1,0:T(8,128)(2,1)} async-done(((bf16[768,5376]{1,0:T(8,128)(2,1)}), bf16[192,5376]{1,0:T(8,128)(2,1)}) %reduce-scatter.12.cloned.1.call-update) | async-done | bytes 2064400 | tf_op jit(solution)/shard_map/reduce_scatter | solution.py:1262
  533.8 0.7 copy-done.12
  534.6 0.6 slice.55
  535.2 0.6 slice.54
  535.8 15.0 %copy.46 = bf16[8,128,5313]{1,0,2:T(8,128)(2,1)} copy(bf16[8,128,5313]{2,1,0:T(8,128)(2,1)} %get-tuple-element.125) | data formatting | bytes 21762048
  550.7 27.6 %back_one.1 = (f32[8,128,1280]{2,1,0:T(8,128)}, f32[8,640]{1,0:T(8,128)}) custom-call(bf16[4,272,768]{2,1,0:T(8,128)(2,1)} %get-tuple-element.85.grad_ext, bf16[768,3200]{1,0:T(8,128)(2,1)} %all-gather.4.cloned.1.call-done.w_one, bf16[8,128,1280]{2,1,0:T(8,128)(2,1)} %get-tuple-element.55.x2, f32[8,1280]{1,0:T(8,128)} %get-tuple-element.86.bn_one, ...), custom_call_target="tpu_custom_call" | custom-call | tf_op jit(solution)/shard_map/back_one/pallas_call | solution.py:1071
  578.4 8.9 %input_grad.1 = bf16[8,256,640]{2,1,0:T(8,128)(2,1)} custom-call(s32[9]{0:T(128)} %pad_add_fusion.1.meta, f32[8,128,1280]{2,1,0:T(8,128)} %get-tuple-element.87.du, bf16[8,128,1280]{2,1,0:T(8,128)(2,1)} %get-tuple-element.55.x2, f32[8,1280]{1,0:T(8,128)} %get-tuple-element.86.bn_one, f32[8,640]{1,0:T(8,128)} %get-tuple-element.88.sums, f32[1,1280]{1,0:T(1,128)} %bitcast.41), custom_call_target="tpu_custom_call" | custom-call | tf_op jit(solution)/shard_map/input_grad/pallas_call | solution.py:1109
  587.3 0.6 slice_reduce_fusion.4
  587.9 0.6 slice_reduce_fusion.2
  588.5 0.6 slice_reduce_fusion
  589.1 62.4 %all-reduce.7.cloned.1.call-done = (bf16[5,640,192]{2,1,0:T(8,128)(2,1)}, bf16[3,192,384]{2,1,0:T(8,128)(2,1)}, bf16[384,192]{0,1:T(8,128)(2,1)}, bf16[192,5376]{1,0:T(8,128)(2,1)}, bf16[192,1792]{1,0:T(8,128)(2,1)}) async-done(((bf16[5,640,192]{2,1,0:T(8,128)(2,1)}, bf16[3,192,384]{2,1,0:T(8,128)(2,1)}, bf16[384,192]{0,1:T(8,128)(2,1)}, bf16[192,5376]{1,0:T(8,128)(2,1)}, bf16[192,1792]{1,0:T(8,128)(2,1)}), ...) | async-done | bytes 4571152 | tf_op jit(solution)/shard_map/psum | solution.py:1263
  651.5 1.7 transpose.26
  653.2 3.6 copy.47
  656.8 1.0 convert_element_type.43
  657.8 1.1 slice_convert_fusion.1
  658.9 2.3 slice_convert_fusion
  (63 shorter events, 0.4 us)
Async XLA Ops:
  7.2 1.0 copy-start
  7.2 67.0 %all-gather.6.cloned.1.call-start = ((), (), s32[]{:S(2)}) async-start(), calls=%async_computation.6 | async-start | bytes 1990656 | tf_op jit(solution)/shard_map/all_gather | solution.py:1175
  8.9 75.0 %all-gather.4.cloned.1.call-start = ((), (), s32[]{:S(2)}) async-start(), calls=%async_computation.5 | async-start | bytes 5529600 | tf_op jit(solution)/shard_map/all_gather | solution.py:1175
  11.8 1.7 copy-start.5
  13.3 2.7 copy-start.19
  13.3 3.2 copy-start.20
  13.3 3.8 copy-start.15
  13.3 4.4 copy-start.16
  13.3 4.9 copy-start.3
  13.3 4.9 copy-start.2
  13.4 8.0 %copy-start.17 = (f32[640]{0:T(1024)S(1)}, f32[640]{0:T(1024)}, u32[]{:S(2)}) copy-start(f32[640]{0:T(1024)} %param.27) | copy-start | bytes 7684
  13.4 8.6 %copy-start.18 = (f32[640]{0:T(1024)S(1)}, f32[640]{0:T(1024)}, u32[]{:S(2)}) copy-start(f32[640]{0:T(1024)} %param.28) | copy-start | bytes 7684
  13.4 9.2 %copy-start.14 = (f32[1643]{0:T(1024)S(1)}, f32[1643]{0:T(1024)}, u32[]{:S(2)}) copy-start(f32[1643]{0:T(1024)} %param.26) | copy-start | bytes 19720
  13.4 9.8 %copy-start.13 = (f32[5313]{0:T(1024)S(1)}, f32[5313]{0:T(1024)}, u32[]{:S(2)}) copy-start(f32[5313]{0:T(1024)} %param.25) | copy-start | bytes 63760
  13.4 141.7 %all-gather.8.cloned.1.call-start = ((), (), s32[]{:S(2)}) async-start(), calls=%async_computation.7 | async-start | bytes 12386304 | tf_op jit(solution)/shard_map/all_gather | solution.py:1175
  15.9 321.0 %reduce-scatter.6.cloned.1.call-start = ((), (), s32[]{:S(2)}) async-start(), calls=%async_computation.8 | async-start | bytes 6144000 | tf_op jit(solution)/shard_map/reduce_scatter | solution.py:1262
  52.5 7.0 %copy-start.11 = (bf16[384,192]{0,1:T(8,128)(2,1)S(1)}, bf16[384,192]{0,1:T(8,128)(2,1)}, u32[]{:S(2)}) copy-start(bf16[384,192]{0,1:T(8,128)(2,1)} %param.22) | copy-start | bytes 442372
  279.2 85.5 %reduce-scatter.10.cloned.1.call-start = ((), (), s32[]{:S(2)}) async-start(), calls=%async_computation.10 | async-start | bytes 737280 | tf_op jit(solution)/shard_map/reduce_scatter | solution.py:1262
  279.7 120.6 %reduce-scatter.8.cloned.1.call-start = ((), (), s32[]{:S(2)}) async-start(), calls=%async_computation.9 | async-start | bytes 2211840 | tf_op jit(solution)/shard_map/reduce_scatter | solution.py:1262
  280.3 164.0 %reduce-scatter.14.cloned.1.call-start = ((), (), s32[]{:S(2)}) async-start(), calls=%async_computation.12 | async-start | bytes 3440640 | tf_op jit(solution)/shard_map/reduce_scatter | solution.py:1262
  281.1 252.7 %reduce-scatter.12.cloned.1.call-start = ((), (), s32[]{:S(2)}) async-start(), calls=%async_computation.11 | async-start | bytes 10321920 | tf_op jit(solution)/shard_map/reduce_scatter | solution.py:1262
  281.8 369.7 %all-reduce.7.cloned.1.call-start = ((), (), s32[]{:S(2)}) async-start(), calls=%async_computation.13 | async-start | bytes 9961472 | tf_op jit(solution)/shard_map/psum | solution.py:1263
  533.8 0.7 copy-start.12
  578.3 9.0 %copy-start.10 = (f32[8,384]{1,0:T(8,128)S(1)}, f32[8,384]{1,0:T(8,128)}, u32[]{:S(2)}) copy-start(f32[8,384]{1,0:T(8,128)} %get-tuple-element.70.sums_three) | copy-start | bytes 36868
  578.4 9.5 %copy-start.9 = (f32[8,640]{1,0:T(8,128)S(1)}, f32[8,640]{1,0:T(8,128)}, u32[]{:S(2)}) copy-start(f32[8,640]{1,0:T(8,128)} %get-tuple-element.88.sums) | copy-start | bytes 61444
  578.4 10.1 %copy-start.8 = (f32[8,768]{1,0:T(8,128)S(1)}, f32[8,768]{1,0:T(8,128)}, u32[]{:S(2)}) copy-start(f32[8,768]{1,0:T(8,128)} %get-tuple-element.79.sums_two) | copy-start | bytes 73732
  651.5 5.3 copy-start.7
  653.2 4.6 copy-start.6
  656.8 2.1 copy-start.4
  658.9 2.3 copy-start.1
Sparse Core Ops, SparseCore 0:
  10.5 29.2 all-gather.5
  42.2 41.7 all-gather.3
  86.4 68.6 all-gather.7
  279.3 57.5 reduce-scatter.5
  339.6 25.0 reduce-scatter.9
  367.9 32.4 reduce-scatter.7
  403.7 40.6 reduce-scatter.13
  448.5 85.2 reduce-scatter.11
  537.4 114.0 all-reduce.6

commit v2 on v1

--- a/solution.py
+++ b/solution.py
@@ -270,6 +270,127 @@
     )(meta, tracks, tracks)
 
 
+class Gathering:
+    STAGES = 5
+
+    def __init__(self, place, shard, full, rows_at, sems):
+        self.place, self.shard, self.full, self.rows_at, self.sems = place, shard, full, rows_at, sems
+        p = place
+        x, y, z = lax.rem(p.dp, 2), lax.div(p.dp, 2), lax.rem(p.seq, 2)
+        self.share = shard.shape[rows_at]
+        self.group = self.share // 6
+        g = self.group
+        self.dp_x, self.dp_y = p.dp + 1 - 2 * x, p.dp + 2 - 4 * y
+        self.dp_xy = 3 - p.dp
+        self.sibling = (1 - p.sec, p.seq, p.dp)
+        self.over_x, self.over_y = (p.sec, p.seq, self.dp_x), (p.sec, p.seq, self.dp_y)
+        self.over_z = (p.sec, p.seq + 1 - 2 * z, p.dp)
+        base = p.sec * 3 * g
+        self.near, self.middle, self.edge, self.far, self.half = (
+            (base + z * g, 2 * g),
+            (base + g, g),
+            (base + 2 * z * g, g),
+            (base + 2 * (1 - z) * g, g),
+            (base, 3 * g),
+        )
+
+    def at(self, ref, dp, span):
+        start, rows = span
+        index = pl.ds(pl.multiple_of(dp * self.share + start, self.group), rows)
+        return ref.at[:, index] if self.rows_at else ref.at[index]
+
+    def remote(self, dp, span, sem, device, source=None):
+        source = self.at(self.full, dp, span) if source is None else source
+        return pltpu.make_async_remote_copy(
+            src_ref=source,
+            dst_ref=self.at(self.full, dp, span),
+            send_sem=self.sems.at[2 * sem],
+            recv_sem=self.sems.at[2 * sem + 1],
+            device_id=device,
+            device_id_type=MESH,
+        )
+
+    def own_copy(self):
+        target = self.at(self.full, self.place.dp, (0, self.share))
+        return pltpu.make_async_copy(self.shard, target, self.sems.at[26])
+
+    def copies(self, stage):
+        me = self.place.dp
+        if stage == 0:
+            own = self.at(self.shard, 0, self.near)
+            return [
+                self.remote(me, self.near, 0, self.over_x, own),
+                self.remote(me, self.near, 1, self.over_y, own),
+            ]
+        if stage == 1:
+            return [
+                self.remote(self.dp_x, self.middle, 2, self.over_y),
+                self.remote(self.dp_y, self.edge, 3, self.over_x),
+                self.remote(self.dp_x, self.edge, 4, self.over_z),
+                self.remote(self.dp_y, self.edge, 5, self.over_z),
+                self.remote(self.dp_x, self.near, 6, self.sibling),
+                self.remote(self.dp_y, self.near, 7, self.sibling),
+            ]
+        if stage == 2:
+            return [
+                self.remote(self.dp_xy, self.edge, 8, self.over_z),
+                self.remote(self.dp_xy, self.near, 9, self.sibling),
+            ]
+        if stage == 3:
+            return [
+                self.remote(self.dp_x, self.far, 10, self.sibling),
+                self.remote(self.dp_y, self.far, 11, self.sibling),
+                self.remote(self.dp_xy, self.far, 12, self.sibling),
+            ]
+        return []
+
+    def start(self, stage):
+        for copy in self.copies(stage):
+            copy.start()
+
+    def arrived(self, stage, which, dp, span):
+        copy = self.copies(stage)[which]
+        pltpu.make_async_remote_copy(
+            src_ref=self.at(self.full, dp, span),
+            dst_ref=self.at(self.full, dp, span),
+            send_sem=self.sems.at[0],
+            recv_sem=self.sems.at[2 * {0: 0, 1: 2, 2: 8, 3: 10}[stage] + 2 * which + 1],
+            device_id=self.sibling,
+            device_id_type=MESH,
+        ).wait_recv()
+
+    def advance(self, stage):
+        if stage == 0:
+            self.own_copy().start()
+        elif stage == 1:
+            self.arrived(0, 0, self.dp_x, self.near)
+            self.arrived(0, 1, self.dp_y, self.near)
+        elif stage == 2:
+            self.arrived(1, 0, self.dp_xy, self.middle)
+            self.arrived(1, 1, self.dp_xy, self.edge)
+        elif stage == 3:
+            self.arrived(1, 2, self.dp_x, self.far)
+            self.arrived(1, 3, self.dp_y, self.far)
+            self.arrived(2, 0, self.dp_xy, self.far)
+        if stage < 4:
+            self.start(stage)
+            return
+        base = (1 - self.place.sec) * 3 * self.group
+        z = lax.rem(self.place.seq, 2)
+        near = (base + z * self.group, 2 * self.group)
+        far = (base + 2 * (1 - z) * self.group, self.group)
+        self.arrived(1, 4, self.dp_x, near)
+        self.arrived(1, 5, self.dp_y, near)
+        self.arrived(2, 1, self.dp_xy, near)
+        self.arrived(3, 0, self.dp_x, far)
+        self.arrived(3, 1, self.dp_y, far)
+        self.arrived(3, 2, self.dp_xy, far)
+        self.own_copy().wait()
+        for stage in range(4):
+            for copy in self.copies(stage):
+                copy.wait_send()
+
+
 def shifted_rows(value, offset, length):
     rows = value.shape[0]
     if offset:
@@ -277,60 +398,76 @@
     return value[:length]
 
 
-def forward_kernel(
-    shape,
-    x2,
-    edge_low,
-    edge_high,
-    stats_in,
-    gain_one,
-    shift_one,
-    gain_two,
-    shift_two,
-    gain_three,
-    shift_three,
-    w_one,
-    w_two,
-    w_point,
-    u_one,
-    u_two,
-    pooled,
-    pooled_low,
-    pooled_high,
-    branch,
-    branch_low,
-    branch_high,
-    act_three,
-    summed,
-    bn_one,
-    bn_two,
-    bn_three,
-    near_one,
-    far_one,
-    s10,
-    s11,
-    s12,
-    s13,
-    near_two,
-    far_two,
-    s20,
-    s21,
-    s22,
-    s23,
-    near_three,
-    far_three,
-    s30,
-    s31,
-    s32,
-    s33,
-    got_low,
-    got_high,
-    stats_two,
-    stats_three,
-    halo_sems,
-    s_branch_edge_low,
-    s_branch_edge_high,
-):
+def forward_kernel(shape, *refs):
+    (
+        x2,
+        edge_low,
+        edge_high,
+        stats_in,
+        gain_one,
+        shift_one,
+        gain_two,
+        shift_two,
+        gain_three,
+        shift_three,
+        in_one,
+        in_two,
+        in_point,
+    ) = refs[:13]
+    refs = refs[13:]
+    (
+        out_u_one,
+        out_u_two,
+        pooled,
+        pooled_low,
+        pooled_high,
+        branch,
+        branch_low,
+        branch_high,
+        act_three,
+        summed,
+        bn_one,
+        bn_two,
+        bn_three,
+        out_one,
+        out_two,
+        out_point,
+    ) = refs[:16]
+    refs = refs[16:]
+    (
+        near_one,
+        far_one,
+        s10,
+        s11,
+        s12,
+        s13,
+        near_two,
+        far_two,
+        s20,
+        s21,
+        s22,
+        s23,
+        near_three,
+        far_three,
+        s30,
+        s31,
+        s32,
+        s33,
+        got_low,
+        got_high,
+        stats_two,
+        stats_three,
+        halo_sems,
+        s_branch_edge_low,
+        s_branch_edge_high,
+        u_one,
+        u_two,
+        w_one,
+        w_two,
+        w_point,
+        weight_sems,
+        save_sems,
+    ) = refs
     place = Place(shape)
     place.greet()
     windows, length, wide = x2.shape
@@ -339,7 +476,37 @@
     small = branch.shape[1]
     parts = shape[0] * shape[1] * shape[2]
     pair = 2 * length
+    saves = [
+        pltpu.make_async_copy(source, target, save_sems.at[i])
+        for i, (source, target) in enumerate(
+            ((u_one, out_u_one), (u_two, out_u_two), (w_one, out_one), (w_two, out_two), (w_point, out_point))
+        )
+    ]
+    gathers = []
+    if in_one.shape[0] < w_one.shape[0]:
+        pieces = [(in_one, w_one, 0), (in_two, w_two, 1), (in_point, w_point, 0)]
+        gathers = [
+            Gathering(place, *piece, weight_sems.at[i]) for i, piece in enumerate(pieces)
+        ]
+    else:
+        loads = [
+            pltpu.make_async_copy(source, target, weight_sems.at[i, 0])
+            for i, (source, target) in enumerate(
+                ((in_one, w_one), (in_two, w_two), (in_point, w_point))
+            )
+        ]
+        for load in loads:
+            load.start()
+        for load in loads:
+            load.wait()
+
+    def advance(*steps):
+        for index, stage in steps:
+            if index < len(gathers):
+                gathers[index].advance(stage)
+
     place.meet()
+    advance((0, 0))
     up, down = halo_copies(place, (edge_low, edge_high), (got_low, got_high), halo_sems.at[0])
     up.start()
     down.start()
@@ -355,6 +522,7 @@
     bn_one[...] = jnp.concatenate([stats, stats], axis=1)
     up.wait()
     down.wait()
+    advance((0, 1), (1, 0), (2, 0))
 
     @pl.loop(0, windows)
     def _(w):
@@ -389,6 +557,10 @@
         for t, tap in enumerate(taps):
             u_one[pl.ds(start, length), t * channels : (t + 1) * channels] = tap.astype(bf16)
 
+    saves[0].start()
+    advance((0, 2), (1, 1), (2, 1), (0, 3), (1, 2), (2, 2), (0, 4))
+    saves[2].start()
+
     @pl.loop(0, MB)
     def _(m):
         start = pl.multiple_of(m * pair, pair)
@@ -417,6 +589,7 @@
     bn_two[...] = finish_stats(stats, pair * parts)
     up.wait()
     down.wait()
+    advance((1, 3), (2, 3))
 
     @pl.loop(0, windows)
     def _(w):
@@ -441,10 +614,19 @@
             tap = shifted_rows(ext, EDGE + (t - 1) * DILATION, length)
             u_two[pl.ds(start, length), t * mid : (t + 1) * mid] = tap.astype(bf16)
 
+    saves[1].start()
+    advance((1, 4), (2, 4))
+    saves[3].start()
+    saves[4].start()
+
     @pl.loop(0, MB)
     def _(m):
         start = pl.multiple_of(m * pair, pair)
-        value = dot_nn(u_two[pl.ds(start, pair), :], w_two[...])
+        value = jnp.zeros((pair, small), f32)
+        for t in range(w_two.shape[0]):
+            value = value + dot_nn(
+                u_two[pl.ds(start, pair), t * mid : (t + 1) * mid], w_two[t]
+            )
         branch[pl.ds(start, pair), :] = value
         centre, spread = local_stats(value)
         stats_three[pl.ds(m, 1), :] = centre
@@ -485,15 +667,22 @@
 
     up.wait()
     down.wait()
-
-
-def forward(shape, x2, edge_low, edge_high, stats, gains, w_one, w_two, w_point):
+    for save in saves:
+        save.wait()
+
+
+def forward(shape, mid, x2, edge_low, edge_high, stats, gains, w_one, w_two, w_point):
     windows, length, wide = x2.shape
     rows = windows * length
-    mid, small = w_point.shape
+    taps_two, _, small = w_two.shape
+    big = [
+        ((mid, w_one.shape[1]), bf16),
+        ((taps_two, mid, small), bf16),
+        ((mid, small), bf16),
+    ]
     out = [
         ((rows, w_one.shape[1]), bf16),
-        ((rows, w_two.shape[0]), bf16),
+        ((rows, taps_two * mid), bf16),
         ((windows, length, mid), bf16),
         ((windows, EDGE, mid), bf16),
         ((windows, EDGE, mid), bf16),
@@ -506,6 +695,8 @@
         ((2 * MB, mid), f32),
         ((2 * MB, small), f32),
     ]
+    out_specs = [HBM] * 2 + [VM] * 11 + [HBM] * 3
+    out += big
     scratch = (
         reduce_scratch(shape, 2 * MB, wide // 2)
         + reduce_scratch(shape, 2 * MB, mid)
@@ -519,11 +710,18 @@
         pltpu.SemaphoreType.DMA((3, 4)),
         pltpu.VMEM((windows, EDGE, small), f32),
         pltpu.VMEM((windows, EDGE, small), f32),
+        pltpu.VMEM(*out[0]),
+        pltpu.VMEM(*out[1]),
+    ]
+    scratch += [pltpu.VMEM(*b) for b in big]
+    scratch += [
+        pltpu.SemaphoreType.DMA((3, 27)),
+        pltpu.SemaphoreType.DMA((5,)),
     ]
     return pl.pallas_call(
         functools.partial(forward_kernel, shape),
-        in_specs=[VM] * 13,
-        out_specs=[VM] * len(out),
+        in_specs=[VM] * 10 + [HBM] * 3,
+        out_specs=out_specs,
         out_shape=[jax.ShapeDtypeStruct(*o) for o in out],
         scratch_shapes=scratch,
         compiler_params=params(1),
@@ -646,7 +844,6 @@
     windows, _, human_tracks = cotangent.shape
     rows, mid = summed.shape
     blocks = w_heads.shape[1] // BLOCK - 1
-    sec_at = 2 * windows + 1
     row_block = pl.BlockSpec((1, BLOCK), lambda j, meta: (0, j))
     row_fixed = pl.BlockSpec((1, BLOCK), lambda j, meta: (0, 0))
     fixed = pl.BlockSpec((rows, mid), lambda j, meta: (0, 0))
@@ -658,10 +855,12 @@
             in_specs=[
                 fixed,
                 pl.BlockSpec((mid, BLOCK), lambda j, meta: (0, j)),
-                pl.BlockSpec((mid, BLOCK), lambda j, meta: (0, blocks), pipeline_mode=pl.Buffered(1)),
+                pl.BlockSpec(
+                    (mid, BLOCK), lambda j, meta: (0, blocks), pipeline_mode=pl.Buffered(1)
+                ),
                 row_block,
                 row_fixed,
-                pl.BlockSpec((windows, length, BLOCK), lambda j, meta: (0, meta[sec_at], j)),
+                pl.BlockSpec((windows, length, BLOCK), lambda j, meta: (0, 0, j)),
             ],
             out_specs=[
                 pl.BlockSpec((windows, length, BLOCK), lambda j, meta: (0, 0, j)),
@@ -888,7 +1087,10 @@
     for move in moves:
         move.start()
     sums_two[...] = reduce_everywhere(place, sums[...], near, far, (s0, s1, s2, s3), add_up)
-    d_two[...] = dot_tn(u_two[...], grad_branch[...]).astype(bf16)
+    small = grad_branch.shape[1]
+    for t in range(taps):
+        part = dot_tn(u_two[:, t * mid : (t + 1) * mid], grad_branch[...])
+        d_two[:, t * small : (t + 1) * small] = part.astype(bf16)
     for move in moves:
         move.wait()
 
@@ -897,7 +1099,7 @@
     windows, length, mid = pooled.shape
     rows, small = branch[0].shape
     out = [
-        (w_two.shape, bf16),
+        ((mid, w_two.shape[0] // mid * small), bf16),
         ((windows, length, mid), f32),
         ((windows, mid), f32),
         ((windows, mid), f32),
@@ -1129,6 +1331,217 @@
     )(meta, du, x2, bn_one, sums, gain)
 
 
+class Summing:
+    STAGES = 7
+
+    def __init__(self, place, source, columns, own, buffers, sems, emit):
+        self.place, self.source, self.columns, self.own = place, source, columns, own
+        self.core, self.side_a, self.side_b, self.end_a, self.end_b = buffers[:5]
+        self.z_near, self.z_far, self.z_back, self.mate = buffers[5:]
+        self.sems, self.emit = sems, emit
+        half = own.shape[2]
+        self.half, self.part = half, half // 2
+        self.mine = pl.ds(pl.multiple_of(place.sec * half, half), half)
+        self.other = pl.ds(pl.multiple_of((1 - place.sec) * half, half), half)
+        self.x, self.y = lax.rem(place.dp, 2), lax.div(place.dp, 2)
+        self.z = lax.rem(place.seq, 2)
+        self.top, self.bottom = pl.ds(0, self.part), pl.ds(self.part, self.part)
+        self.keep = pl.ds(pl.multiple_of(self.z * self.part, self.part), self.part)
+        self.give = pl.ds(pl.multiple_of((1 - self.z) * self.part, self.part), self.part)
+
+    def remote(self, source, target, sem, device):
+        return pltpu.make_async_remote_copy(
+            src_ref=source,
+            dst_ref=target,
+            send_sem=self.sems.at[2 * sem],
+            recv_sem=self.sems.at[2 * sem + 1],
+            device_id=device,
+            device_id_type=MESH,
+        )
+
+    def copies(self, stage):
+        p, own, x, y = self.place, self.own, self.x, self.y
+        sibling = (1 - p.sec, p.seq, p.dp)
+        over_x = (p.sec, p.seq, p.dp + 1 - 2 * x)
+        over_y = (p.sec, p.seq, p.dp + 2 - 4 * y)
+        over_z = (p.sec, p.seq + 1 - 2 * self.z, p.dp)
+        z_pair = lax.div(p.seq, 2)
+        beyond = (p.sec, p.seq + 2 - 4 * z_pair, p.dp)
+        if stage == 0:
+            return [
+                pltpu.make_async_copy(
+                    self.source.at[:, :, self.mine, self.columns], own, self.sems.at[20]
+                ),
+                self.remote(
+                    self.source.at[:, :, self.other, self.columns], self.core, 0, sibling
+                ),
+            ]
+        if stage == 1:
+            return [
+                self.remote(own.at[:, 1 - x, self.top], self.side_a, 1, over_x),
+                self.remote(own.at[1 - y, :, self.bottom], self.side_b, 2, over_y),
+            ]
+        if stage == 2:
+            return [
+                self.remote(own.at[1 - y, x, self.top], self.end_a, 3, over_y),
+                self.remote(own.at[y, 1 - x, self.bottom], self.end_b, 4, over_x),
+            ]
+        if stage == 3:
+            return [self.remote(own.at[y, x, self.give], self.z_near, 5, over_z)]
+        if stage == 4:
+            return [self.remote(own.at[y, x, self.keep], self.z_far, 6, beyond)]
+        if stage == 5:
+            return [self.remote(own.at[y, x, self.keep], self.z_back, 7, over_z)]
+        return [
+            self.remote(own.at[y, x, self.keep], self.mate.at[self.keep], 8, sibling),
+            self.remote(self.z_back, self.mate.at[self.give], 9, sibling),
+        ]
+
+    def start(self, stage):
+        for copy in self.copies(stage):
+            copy.start()
+
+    def finish(self, stage):
+        for copy in self.copies(stage):
+            copy.wait()
+        own, x, y = self.own, self.x, self.y
+
+        def add(at, other):
+            own[at] = (own[at].astype(f32) + other.astype(f32)).astype(bf16)
+
+        if stage == 0:
+
+            @pl.loop(0, 4)
+            def _(i):
+                a, b = lax.div(i, 2), lax.rem(i, 2)
+                add((a, b), self.core[a, b])
+
+        elif stage == 1:
+            for i in range(2):
+                add((i, x, self.top), self.side_a[i])
+                add((y, i, self.bottom), self.side_b[i])
+        elif stage == 2:
+            add((y, x, self.top), self.end_a[...])
+            add((y, x, self.bottom), self.end_b[...])
+        elif stage == 3:
+            add((y, x, self.keep), self.z_near[...])
+        elif stage == 4:
+            add((y, x, self.keep), self.z_far[...])
+        elif stage == 6:
+            base = self.place.sec * self.half
+            there = (1 - self.place.sec) * self.half
+            first = pl.multiple_of(base + self.z * self.part, self.part)
+            second = pl.multiple_of(base + (1 - self.z) * self.part, self.part)
+            self.emit(first, self.part, own[y, x, self.keep].astype(f32))
+            self.emit(second, self.part, self.z_back[...].astype(f32))
+            self.emit(pl.multiple_of(there, self.half), self.half, self.mate[...].astype(f32))
+
+    @staticmethod
+    def scratch(share, width):
+        half = share // 2
+        part = half // 2
+        return [
+            pltpu.VMEM((2, 2, half, width), bf16),
+            pltpu.VMEM((2, 2, half, width), bf16),
+            pltpu.VMEM((2, part, width), bf16),
+            pltpu.VMEM((2, part, width), bf16),
+            pltpu.VMEM((part, width), bf16),
+            pltpu.VMEM((part, width), bf16),
+            pltpu.VMEM((part, width), bf16),
+            pltpu.VMEM((part, width), bf16),
+            pltpu.VMEM((part, width), bf16),
+            pltpu.VMEM((half, width), bf16),
+            pltpu.SemaphoreType.DMA((21,)),
+        ]
+
+
+def grad_chunks(human_tracks, mouse_tracks, channels, mid, small):
+    chunks = []
+    for start in range(0, human_tracks, BLOCK):
+        width = min(BLOCK, human_tracks - start)
+        chunks.append((0, start, BLOCK, [(0, None, start, 0, width)]))
+    chunks.append((1, 0, BLOCK, [(1, None, 0, 0, mouse_tracks)]))
+    chunks.append((2, 0, small, [(2, None, 0, 0, small)]))
+    chunks.append((3, 0, 3 * small, [(3, t, 0, t * small, small) for t in range(3)]))
+    for taps in ((0, 1, 2), (3, 4)):
+        chunks.append(
+            (
+                4,
+                taps[0] * channels,
+                len(taps) * channels,
+                [(4, t, 0, i * channels, channels) for i, t in enumerate(taps)],
+            )
+        )
+    return chunks
+
+
+def sum_kernel(shape, chunks, n_in, *refs):
+    sources, refs = refs[:n_in], refs[n_in:]
+    outs, refs = refs[:n_in], refs[n_in:]
+    place = Place(shape)
+    place.greet()
+    place.meet()
+    sums = []
+    for index, (source, start, width, targets) in enumerate(chunks):
+        scratch, refs = refs[:11], refs[11:]
+
+        def emit(row, rows, value, targets=targets):
+            for out, tap, to, at, columns in targets:
+                piece = value[:, at : at + columns]
+                if tap is None:
+                    outs[out][pl.ds(row, rows), to : to + columns] = piece
+                else:
+                    outs[out][tap, pl.ds(row, rows), to : to + columns] = piece
+
+        sums.append(
+            Summing(
+                place,
+                sources[source],
+                pl.ds(start, width),
+                scratch[0],
+                scratch[1:10],
+                scratch[10],
+                emit,
+            )
+        )
+    count = len(sums)
+    lag = [-2, -1, 0, 1, 2, 3, 4]
+    for tick in range(-2, count + Summing.STAGES):
+        for stage in range(Summing.STAGES + 1):
+            k = tick - lag[stage] if stage < Summing.STAGES else tick - lag[-1] - 1
+            if 0 <= k < count:
+                if stage > 0:
+                    sums[k].finish(stage - 1)
+                if stage < Summing.STAGES:
+                    sums[k].start(stage)
+
+
+def sum_grads(shape, grads, human_tracks, mouse_tracks, channels):
+    mid = grads[0].shape[0]
+    small = grads[2].shape[1]
+    share = mid // shape[2]
+    taps_one = grads[4].shape[1] // channels
+    chunks = grad_chunks(human_tracks, mouse_tracks, channels, mid, small)
+    scratch = []
+    for chunk in chunks:
+        scratch += Summing.scratch(share, chunk[2])
+    return pl.pallas_call(
+        functools.partial(sum_kernel, shape, chunks, len(grads)),
+        in_specs=[HBM] * len(grads),
+        out_specs=[VM] * len(grads),
+        out_shape=[
+            jax.ShapeDtypeStruct((share, human_tracks), f32),
+            jax.ShapeDtypeStruct((share, mouse_tracks), f32),
+            jax.ShapeDtypeStruct((share, small), f32),
+            jax.ShapeDtypeStruct((3, share, small), f32),
+            jax.ShapeDtypeStruct((taps_one, share, channels), f32),
+        ],
+        scratch_shapes=scratch,
+        compiler_params=params(5),
+        name="sum_grads",
+    )(*[g.reshape(2, 2, share, g.shape[1]) for g in grads])
+
+
 def per_device(
     shape,
     tracks,
@@ -1168,16 +1581,12 @@
         ],
         axis=1,
     )
-
-    def gathered(shard, axis):
-        size = shard.shape[axis] // 2
-        part = lax.dynamic_slice_in_dim(shard, sec * size, size, axis)
-        return lax.all_gather(part, ("dp", "section"), axis=axis, tiled=True)
-
-    w_one = gathered(shard_one, 0)
-    w_two = gathered(dilated_kernel, 1).reshape(-1, dilated_kernel.shape[2])
-    w_point = gathered(shard_point, 0)
-    w_heads = gathered(shard_heads, 0)
+    half_rows = share // shape[0]
+    half_heads = lax.dynamic_slice_in_dim(shard_heads, sec * half_rows, half_rows, 0)
+    w_heads = lax.all_gather(half_heads, ("dp", "section"), axis=0, tiled=True)
+    weights = [shard_one, dilated_kernel, shard_point]
+    if shape != (2, 4, 4):
+        weights = [lax.all_gather(w, "dp", axis=w.ndim - 2, tiled=True) for w in weights]
 
     meta_one = jnp.concatenate([batch_order, sec[None]])
     x2, edge_low, edge_high, stats = prepare(tracks, meta_one, half)
@@ -1205,7 +1614,11 @@
         bn_one,
         bn_two,
         bn_three,
-    ) = forward(shape, x2, edge_low, edge_high, stats, gains, w_one, w_two, w_point)
+        w_one,
+        w_two,
+        w_point,
+    ) = forward(shape, mid, x2, edge_low, edge_high, stats, gains, *weights)
+    w_two = w_two.reshape(-1, w_two.shape[2])
 
     kinds = species[batch_order]
     is_human = kinds == 0
@@ -1222,8 +1635,9 @@
     ).astype(jnp.int32)
     wide_human = jnp.pad(bias_human, (0, human_wide - human_tracks)).reshape(1, -1)
     wide_mouse = jnp.pad(bias_mouse, (0, BLOCK - mouse_tracks)).reshape(1, -1)
+    cot_half = lax.dynamic_slice_in_dim(cotangent, sec * length, length, 1)
     predicted, grad_summed, d_human, d_mouse, db_human, db_mouse = heads(
-        meta_two, summed, w_heads, wide_human, wide_mouse, cotangent, mouse_tracks, length
+        meta_two, summed, w_heads, wide_human, wide_mouse, cot_half, mouse_tracks, length
     )
 
     bias_sums = jnp.concatenate([db_human, db_mouse], axis=1).reshape(8, -1)
@@ -1258,15 +1672,23 @@
     du_one, sums_one = back_one(shape, grad_ext, w_one, x2, bn_one, gains[0], gains[1])
     grad_input = input_grad(shape, meta_one, du_one, x2, bn_one, sums_one, gains[0])
 
-    def reduced(grad, axis):
-        part = lax.psum_scatter(grad, "dp", scatter_dimension=axis, tiled=True)
-        return lax.psum(part, ("section", "seq")).astype(f32)
-
-    r_human = reduced(d_human, 0)[:, :human_tracks]
-    r_mouse = reduced(d_mouse, 0)[:, :mouse_tracks]
-    r_two = reduced(d_two.reshape((dilated_kernel.shape[0], mid, -1)), 1)
-    r_point = reduced(d_point, 0).T
-    r_one = jnp.transpose(reduced(d_one, 0).reshape(share, taps_one, channels), (1, 2, 0))
+    grads = (d_human, d_mouse, d_point, d_two, d_one)
+    if shape == (2, 4, 4):
+        r_human, r_mouse, r_point, r_two, r_one = sum_grads(
+            shape, grads, human_tracks, mouse_tracks, channels
+        )
+    else:
+
+        def reduced(grad):
+            part = lax.psum_scatter(grad, "dp", scatter_dimension=0, tiled=True)
+            return lax.psum(part, ("section", "seq")).astype(f32)
+
+        r_human, r_mouse, r_point, r_two, r_one = [reduced(grad) for grad in grads]
+        r_human, r_mouse = r_human[:, :human_tracks], r_mouse[:, :mouse_tracks]
+        r_two = jnp.transpose(r_two.reshape(share, -1, dilated_kernel.shape[2]), (1, 0, 2))
+        r_one = jnp.transpose(r_one.reshape(share, taps_one, channels), (1, 0, 2))
+    r_point = r_point.T
+    r_one = jnp.transpose(r_one, (0, 2, 1))
     bias = bias_out.reshape(-1)
     return (
         predicted,

time: 679 us -> 464 us (0.68)
  waiting for transfers between devices: 337 us -> 0.02 us
  Pallas kernels: 223 us -> 374 us
  blocking collectives: 14.6 us -> 0 us
    reduce_scatter x5 -> x0, waiting for transfers between devices: 249 us -> none  [reduced(): part = lax.psum_scatter(grad, 'dp', scatter_dimension=axis, tiled=True)]
    pallas_call x0 -> x1, Pallas kernels: none -> 119 us  [sum_grads(): pl.pallas_call(functools.partial(sum_kernel, shape, chunks, len(grads)),...]
    psum x1 -> x0, waiting for transfers between devices: 62.4 us -> none  [reduced(): return lax.psum(part, ('section', 'seq')).astype(f32)]
    pallas_call x1, Pallas kernels: 57.7 us -> 87.7 us  [forward(): pl.pallas_call(functools.partial(forward_kernel, shape), in_specs=[VM] *...]
    all_gather x3 -> x1, waiting for transfers between devices: 23.2 us -> 0.01 us  [per_device(): w_heads = lax.all_gather(half_heads, ('dp', 'section'), axis=0, tiled=True)]
    all_gather x1 -> x0, blocking collectives: 14.6 us -> none  [gathered(): return lax.all_gather(part, ('dp', 'section'), axis=axis, tiled=True)]
    unnamed x50 -> x45, local copies, waits for them, and re-layouts: 50.7 us -> 38.9 us
    dynamic_slice x3 -> x1, local copies, waits for them, and re-layouts: 1.04 us -> 9.64 us  [per_device(): cot_half = lax.dynamic_slice_in_dim(cotangent, sec * length, length, 1)]
  transfers between devices with their start and end apart: 9 -> 1, of which waited for: 8 -> 0; matrix products, arithmetic and copies ran while one was open for 10% -> 8% of each run, Pallas kernels for 15% -> 20%
where the time goes in v2:
time: 464 us; the launch traced here: 459 us
  Pallas kernels  374 us (81%)
  local copies, waits for them, and re-layouts  59.4 us (13%)
  between operations  14.5 us (3%)
  other arithmetic  10.5 us (2%)
    pallas_call x1, Pallas kernels, sum_grads(): pl.pallas_call(functools.partial(sum_kernel, shape, chunks, len(grads)),...  119 us
    pallas_call x1, Pallas kernels, forward(): pl.pallas_call(functools.partial(forward_kernel, shape), in_specs=[VM] *...  87.7 us
    pallas_call x1, Pallas kernels, heads(): pl.pallas_call(functools.partial(heads_kernel, human_tracks, mouse_tracks...  65.5 us
    unnamed x45, local copies, waits for them, and re-layouts  38.9 us
    pallas_call x1, Pallas kernels, back_one(): pl.pallas_call(functools.partial(back_one_kernel, shape), in_specs=[VM] *...  26.2 us
    pallas_call x1, Pallas kernels, back_three(): pl.pallas_call(functools.partial(back_three_kernel, shape), in_specs=[VM]...  24.2 us
    pallas_call x1, Pallas kernels, back_two(): pl.pallas_call(functools.partial(back_two_kernel, shape), in_specs=[VM] *...  23.1 us
    pallas_call x1, Pallas kernels, pool_grad(): pl.pallas_call(functools.partial(pool_grad_kernel, shape), in_specs=[VM]...  14.3 us
  transfers between devices with their start and end apart: 1, of which 0 were waited for; matrix products, arithmetic and copies ran while one was open for 8% of the time, Pallas kernels for 20%

profile of v2, /device:TPU:0, one launch (start us, length us, event | category | flops | bytes accessed | tf_op | source)
XLA Modules:
  0.0 458.7 jit_solution(8628145242763887075)
XLA Ops:
  7.2 0.0 copy-start
  7.2 0.0 copy-start.15
  7.2 0.0 copy-start.16
  7.2 0.0 copy-start.12
  7.2 0.0 copy-start.13
  7.2 0.0 copy-start.3
  7.3 0.0 all-gather.2.cloned.1.call-start
  7.3 0.0 copy-start.2
  7.3 0.0 copy-start.14
  7.4 2.6 fusion.2
  9.9 0.0 all-gather.2.cloned.1.call-update
  10.0 0.0 copy-done.15
  10.0 0.6 reshape.166.refs_8_.gain_three
  10.5 0.6 reshape.167.refs_9_.shift_three
  11.1 0.6 reshape.164.refs_6_.gain_two
  11.7 0.6 reshape.165.refs_7_.shift_two
  12.3 0.0 copy-done.2
  12.3 0.6 gather_fusion
  13.0 0.2 reduce-window.17
  13.1 0.2 reduce-window.16
  13.3 0.6 fusion.4
  14.0 0.6 compare_select_fusion.2
  14.6 0.1 select_reduce_fusion
  14.8 0.6 gather_fusion.1
  15.4 0.0 copy-done
  15.4 0.6 copy.44
  16.0 0.6 copy.45
  16.6 0.0 copy-done.11
  16.6 0.6 reshape.170.b_mouse
  17.2 0.6 reshape.169.b_human
  17.9 1.9 copy.39
  19.7 1.6 copy.40.refs_10_
  21.4 9.6 %constant_dynamic-slice_fusion = bf16[8,128,5313]{1,0,2:T(8,128)(2,1)} fusion(bf16[8,256,5313]{1,0,2:T(8,128)(2,1)} %param.33, s32[]{:T(128)S(6)} %select_n.36), kind=kLoop, calls=%fused_computation.26 | loop fusion | bytes 21762052 | tf_op jit(solution)/shard_map/dynamic_slice | solution.py:1638
  31.0 14.6 %copy.43.cot = bf16[8,128,5313]{2,1,0:T(8,128)(2,1)} copy(bf16[8,128,5313]{1,0,2:T(8,128)(2,1)} %constant_dynamic-slice_fusion) | data formatting | bytes 21762048
  45.6 0.6 pad_add_fusion.1.meta
  46.2 5.7 %prepare.1 = (bf16[8,128,1280]{2,1,0:T(8,128)(2,1)}, f32[8,1280]{1,0:T(8,128)}, f32[8,1280]{1,0:T(8,128)}, f32[8,640]{1,0:T(8,128)}) custom-call(s32[9]{0:T(128)} %pad_add_fusion.1.meta, bf16[8,512,640]{2,1,0:T(8,128)(2,1)} %second.1, bf16[8,512,640]{2,1,0:T(8,128)(2,1)} %second.1), custom_call_target="tpu_custom_call" | custom-call | tf_op jit(solution)/shard_map/prepare/pallas_call | solution.py:245
  51.9 87.7 %forward.1 = (bf16[1024,3200]{1,0:T(8,128)(2,1)}, bf16[1024,2304]{1,0:T(8,128)(2,1)}, bf16[8,128,768]{2,1,0:T(8,128)(2,1)}, bf16[8,16,768]{2,1,0:T(8,128)(2,1)},...) custom-call(bf16[8,128,1280]{2,1,0:T(8,128)(2,1)} %get-tuple-element, ...), custom_call_target="tpu_custom_call" | custom-call | tf_op jit(solution)/shard_map/forward/pallas_call | solution.py:721
  139.6 1.2 pad_add_fusion.meta
  140.8 65.5 %heads.1 = (bf16[8,128,5313]{2,1,0:T(8,128)(2,1)}, f32[1024,768]{1,0:T(8,128)}, bf16[768,5376]{1,0:T(8,128)(2,1)}, bf16[768,1792]{1,0:T(8,128)(2,1)}, f32[1,5376]{1,0:T(1,128)}, /*index=5*/f32[1,1792]{1,0:T(1,128)}) custom-call(s32[18]{0:T(128)} %pad_add_fusion.meta, bf16[1024,768]{1,0:T(8,128)(2,1)} %get-tuple-element.67.summed, ...), custom_call_target="tpu_custom_call" | custom-call | tf_op jit(solution)/shard_map/heads/pallas_call | solution.py:850
  206.3 0.8 maximum_reduce_fusion
  207.1 0.6 reshape.171.bias_sums
  207.8 24.2 %back_three.1 = (bf16[768,384]{1,0:T(8,128)(2,1)}, f32[1024,384]{1,0:T(8,128)}, f32[8,16,384]{2,1,0:T(8,128)}, f32[8,16,384]{2,1,0:T(8,128)}, f32[8,768]{1,0:T(8...) custom-call(f32[1024,768]{1,0:T(8,128)} %get-tuple-element.69.grad_summed, ...), custom_call_target="tpu_custom_call" | custom-call | tf_op jit(solution)/shard_map/back_three/pallas_call | solution.py:988
  232.0 0.8 reshape.178
  232.8 0.6 slice.37
  233.4 0.6 slice.36
  234.0 14.7 %copy.42 = bf16[8,128,5313]{1,0,2:T(8,128)(2,1)} copy(bf16[8,128,5313]{2,1,0:T(8,128)(2,1)} %get-tuple-element.141) | data formatting | bytes 21762048
  248.7 0.6 slice_reduce_fusion.4
  249.3 23.1 %back_two.1 = (bf16[768,1152]{1,0:T(8,128)(2,1)}, f32[8,128,768]{2,1,0:T(8,128)}, f32[8,768]{1,0:T(8,128)}, f32[8,768]{1,0:T(8,128)}, f32[8,768]{1,0:T(8,128)}) custom-call(f32[1024,384]{1,0:T(8,128)} %get-tuple-element.76.du_three, f32[8,16,384]{2,1,0:T(8,128)} %get-tuple-element.77.du_low, f32[8,16,384]{2,1,0:T(8,128)} %get-tuple-element.78.du_high, ...), custom_call_target="tpu_custom_call" | custom-call | tf_op jit(solution)/shard_map/back_two/pallas_call | solution.py:1116
  272.3 1.4 slice_reduce_fusion
  273.8 14.3 %pool_grad.1 = (bf16[4,272,768]{2,1,0:T(8,128)(2,1)}, bf16[768,3200]{1,0:T(8,128)(2,1)}) custom-call(f32[8,128,768]{2,1,0:T(8,128)} %get-tuple-element.86.du_two, f32[8,768]{1,0:T(8,128)} %get-tuple-element.87.du_low, f32[8,768]{1,0:T(8,128)} %get-tuple-element.88.du_high, f32[8,768]{1,0:T(8,128)} %get-tuple-element.89.sums_two, ...), custom_call_target="tpu_custom_call" | custom-call | tf_op jit(solution)/shard_map/pool_grad/pallas_call | solution.py:1195
  288.1 26.2 %back_one.1 = (f32[8,128,1280]{2,1,0:T(8,128)}, f32[8,640]{1,0:T(8,128)}) custom-call(bf16[4,272,768]{2,1,0:T(8,128)(2,1)} %get-tuple-element.95.grad_ext, bf16[768,3200]{1,0:T(8,128)(2,1)} %get-tuple-element.96.w_one, bf16[8,128,1280]{2,1,0:T(8,128)(2,1)} %get-tuple-element.63.refs_0_.x2, f32[8,1280]{1,0:T(8,128)} %get-tuple-element.97.bn_one, ...), custom_call_target="tpu_custom_call" | custom-call | tf_op jit(solution)/shard_map/back_one/pallas_call | solution.py:1273
  314.2 1.4 slice_reduce_fusion.2
  315.6 8.7 %input_grad.1 = bf16[8,256,640]{2,1,0:T(8,128)(2,1)} custom-call(s32[9]{0:T(128)} %pad_add_fusion.1.meta, f32[8,128,1280]{2,1,0:T(8,128)} %get-tuple-element.98.du, bf16[8,128,1280]{2,1,0:T(8,128)(2,1)} %get-tuple-element.63.refs_0_.x2, f32[8,1280]{1,0:T(8,128)} %get-tuple-element.97.bn_one, f32[8,640]{1,0:T(8,128)} %get-tuple-element.99.sums, ...), custom_call_target="tpu_custom_call" | custom-call | tf_op jit(solution)/shard_map/input_grad/pallas_call | solution.py:1311
  324.3 118.9 %sum_grads.1 = (f32[192,5313]{1,0:T(8,128)}, f32[192,1643]{1,0:T(8,128)}, f32[192,384]{1,0:T(8,128)}, f32[3,192,384]{2,1,0:T(8,128)}, f32[5,192,640]{2,1,0:T(8,128)}) custom-call(bf16[2,2,192,5376]{3,2,1,0:T(8,128)(2,1)} %bitcast.33, bf16[2,2,192,1792]{3,2,1,0:T(8,128)(2,1)} %bitcast.36, bf16[2,2,192,384]{3,2,1,0:T(8,128)(2,1)} %bitcast.41, ...), custom_call_target="tpu_custom_call" | custom-call | tf_op jit(solution)/shard_map/sum_grads/pallas_call | solution.py:1528
  443.2 0.0 copy-start.7
  443.2 0.0 copy-start.8
  443.2 0.0 copy-start.4
  443.2 3.4 copy.51
  446.7 0.9 copy.52
  447.6 0.0 copy-done.8
  447.6 0.7 copy.53
  448.3 2.0 copy.54
  450.3 0.2 copy-done.5
  450.5 1.0 copy.55
  (28 shorter events, 0.1 us)
Async XLA Ops:
  7.2 8.2 %copy-start = (f32[640]{0:T(1024)S(1)}, f32[640]{0:T(1024)}, u32[]{:S(2)}) copy-start(f32[640]{0:T(1024)} %param.27) | copy-start | bytes 7684
  7.2 2.8 copy-start.15
  7.2 3.3 copy-start.16
  7.2 3.9 copy-start.12
  7.2 4.5 copy-start.13
  7.2 5.0 %copy-start.3 = (s32[8]{0:T(128)S(1)}, s32[8]{0:T(128)}, u32[]{:S(2)}) copy-start(s32[8]{0:T(128)} %param.19) | copy-start | bytes 100
  7.3 133.6 %all-gather.2.cloned.1.call-start = ((), (), s32[]{:S(2)}) async-start(), calls=%async_computation | async-start | bytes 12386304 | tf_op jit(solution)/shard_map/all_gather | solution.py:1586
  7.3 5.0 %copy-start.2 = (s32[8]{0:T(128)S(1)}, s32[8]{0:T(128)}, u32[]{:S(2)}) copy-start(s32[8]{0:T(128)} %param.18) | copy-start | bytes 100
  7.3 8.7 %copy-start.14 = (f32[640]{0:T(1024)S(1)}, f32[640]{0:T(1024)}, u32[]{:S(2)}) copy-start(f32[640]{0:T(1024)} %param.28) | copy-start | bytes 7684
  7.3 9.3 %copy-start.11 = (f32[1643]{0:T(1024)S(1)}, f32[1643]{0:T(1024)}, u32[]{:S(2)}) copy-start(f32[1643]{0:T(1024)} %param.26) | copy-start | bytes 19720
  7.3 9.9 %copy-start.10 = (f32[5313]{0:T(1024)S(1)}, f32[5313]{0:T(1024)}, u32[]{:S(2)}) copy-start(f32[5313]{0:T(1024)} %param.25) | copy-start | bytes 63760
  7.3 10.5 %copy-start.6 = (bf16[5,640,192]{1,2,0:T(8,128)(2,1)S(1)}, bf16[5,640,192]{1,2,0:T(8,128)(2,1)}, u32[]{:S(2)}) copy-start(bf16[5,640,192]{1,2,0:T(8,128)(2,1)} %param.20) | copy-start | bytes 3686404
  234.0 14.7 %copy-start.9 = (f32[8,384]{1,0:T(8,128)S(1)}, f32[8,384]{1,0:T(8,128)}, u32[]{:S(2)}) copy-start(f32[8,384]{1,0:T(8,128)} %get-tuple-element.79.sums_three) | copy-start | bytes 36868
  443.2 3.5 copy-start.7
  443.2 4.4 copy-start.8
  443.2 5.1 %copy-start.4 = (f32[192,5313]{1,0:T(8,128)S(1)}, f32[192,5313]{1,0:T(8,128)}, u32[]{:S(2)}) copy-start(f32[192,5313]{1,0:T(8,128)} %get-tuple-element.182) | copy-start | bytes 12241156
  448.3 2.2 copy-start.5
  448.3 3.3 copy-start.1
Sparse Core Ops, SparseCore 0:
  10.5 79.1 all-gather.1
